TPU v7x, 512 devices: a whole 4x8x8 slice. The times are simulated.
512 devices in a mesh: mem: 8 (over z), lat: 32 (over y, x), rep: 2 (over core).
Axes of the slice: x: 4, y: 8, z: 8, core: 2. Of those that a mesh axis runs over, the one named last changes fastest.
Arguments:
- latent: bfloat16 [80, 16384, 256], P(('rep', 'mem'), 'lat'), parts along dimension 0, may hold values from -6 to 6
- in_weight: bfloat16 [256, 1024], replicated, may hold values from -0.375 to 0.375
- in_bias: float32 [1024], replicated, may hold values from -3 to 3
- out_weight: bfloat16 [4, 1024], replicated, may hold values from -0.1875 to 0.1875
- out_bias: float32 [4], replicated, may hold values from -3 to 3
- observed: float32 [8, 16384], P('rep', 'lat'), parts along dimension 0, may hold values from -6 to 6
- patch_of_cell: int32 [16384], P('lat'), may hold values from 0 to 7, as said below
Outputs:
- d_latent: bfloat16 [80, 16384, 256], P(('rep', 'mem'), 'lat'), parts along dimension 0
- d_in_weight: float32 [512, 1024], P('rep'), parts along dimension 0
- d_out_weight: float32 [8, 1024], P('rep'), parts along dimension 0
- d_in_bias: float32 [2048], P('rep'), parts along dimension 0
- d_out_bias: float32 [8], P('rep'), parts along dimension 0
There are 2 independent parts, one for each index of `rep`. A program takes and returns all parts, laid end to end along the dimension named above; an argument that names none is the same for every part. Nothing has to cross between parts.
Inputs may be any that keep to these rules, and one draw needn't show every extreme that they name: `patch_of_cell`: each of the 8 patches holds exactly 2048 cells; patches 2 g and 2 g + 1 together hold exactly the cells 8 g * 512 to 8 (g + 1) * 512 - 1.
All inputs are finite; a program needn't handle non-finite values.
Results may differ from a plain program's by a relative error of at most 0.0025.
The roundings to bfloat16 on the way count: a program that leaves them out, or rounds other values in their place, can miss the bound.
Values may be sent and summed in bfloat16 or wider, within the bound.
No kernel may reach another device: no remote copies, remote signals or barrier semaphores. Data moves between devices by JAX's collectives and lax.ppermute only.
A program may use at most 64 MiB of HBM per device.

v0:
```python
import jax
import jax.numpy as jnp
from jax import lax
from jax.sharding import PartitionSpec as P

epsilon = 1e-06


def local(latent, in_weight, in_bias, out_weight, out_bias, observed, patch_of_cell):
    members_here, cells_here, width = latent.shape
    n_mem = lax.axis_size("mem")
    n_lat = lax.axis_size("lat")
    members = members_here * n_mem
    patches = n_lat // 4
    nvars = out_weight.shape[0]
    entries = float(nvars * 4 * cells_here)
    highest = lax.Precision.HIGHEST
    preact = (
        jnp.einsum("mcd,dk->mck", latent, in_weight, preferred_element_type=jnp.float32) + in_bias
    )
    hidden = jax.nn.silu(preact).astype(jnp.bfloat16)
    field = (
        jnp.einsum("mck,vk->mvc", hidden, out_weight, preferred_element_type=jnp.float32)
        + out_bias[None, :, None]
    ).astype(jnp.bfloat16)
    in_patch = (patch_of_cell[:, None] == jnp.arange(patches, dtype=jnp.int32)[None, :]).astype(
        jnp.float32
    )
    own_field = field.astype(jnp.float32)
    misfit = own_field - observed[None]
    obs_part = jnp.dot(jnp.sum(misfit * misfit, axis=1), in_patch, precision=highest)
    all_fields = lax.all_gather(field, "mem", axis=0, tiled=True)
    diff = own_field[:, None] - all_fields.astype(jnp.float32)[None]
    squared = jnp.sum(diff * diff, axis=2)
    pair_part = jnp.einsum("mnc,cp->mnp", squared, in_patch, precision=highest)
    pair_sum, obs_sum = lax.psum((pair_part, obs_part), "lat")
    spread = jnp.sqrt(obs_sum / entries + epsilon)
    dist = jnp.sqrt(pair_sum / entries + epsilon)
    own_ids = lax.axis_index("mem") * members_here + jnp.arange(members_here, dtype=jnp.int32)
    other_ids = jnp.arange(members, dtype=jnp.int32)
    inv_dist = jnp.where(
        (own_ids[:, None] != other_ids[None, :])[:, :, None], 1.0 / dist, jnp.float32(0.0)
    )
    cell_w = jnp.einsum("mnp,cp->mnc", inv_dist, in_patch, precision=highest)
    cell_spread = jnp.einsum("mp,cp->mc", spread, in_patch, precision=highest)
    row_total = jnp.sum(cell_w, axis=1)
    weighted = jnp.einsum("mnc,nvc->mvc", cell_w, all_fields.astype(jnp.float32), precision=highest)
    grad_field = (
        misfit / cell_spread[:, None, :] - (own_field * row_total[:, None, :] - weighted) / members
    ).astype(jnp.bfloat16)
    d_hidden = jnp.einsum("mvc,vk->mck", grad_field, out_weight, preferred_element_type=jnp.float32)
    gate_sig = jax.nn.sigmoid(preact)
    d_preact = (d_hidden * gate_sig * (1.0 + preact * (1.0 - gate_sig))).astype(jnp.bfloat16)
    d_latent = jnp.einsum(
        "mck,dk->mcd", d_preact, in_weight, preferred_element_type=jnp.float32
    ).astype(jnp.bfloat16)
    out_part = jnp.einsum("mvc,mck->vk", grad_field, hidden, preferred_element_type=jnp.float32)
    bin_part = jnp.sum(d_preact, axis=(0, 1), dtype=jnp.float32)
    bout_part = jnp.sum(grad_field, axis=(0, 2), dtype=jnp.float32)
    in_part = jnp.einsum("mcd,mck->dk", latent, d_preact, preferred_element_type=jnp.float32)
    d_in, d_out, d_bin, d_bout = lax.psum((in_part, out_part, bin_part, bout_part), ("mem", "lat"))
    scale = 1.0 / jnp.sqrt(jnp.float32(members * cells_here * n_lat))
    return (d_latent, d_in * scale, d_out * scale, d_bin * scale, d_bout * scale)


def solution(mesh):
    placed = (P(("rep", "mem"), "lat", None), P(), P(), P(), P(), P("rep", "lat"), P("lat"))
    return jax.shard_map(
        local,
        mesh=mesh,
        in_specs=placed,
        out_specs=(
            P(("rep", "mem"), "lat", None),
            P("rep", None),
            P("rep", None),
            P("rep"),
            P("rep"),
        ),
        check_vma=False,
    )
```

profile of v0, /device:TPU:0, one launch (start us, length us, event | category | flops | bytes accessed | tf_op | source)
XLA Modules:
  0.0 1594.3 jit_solution(1750784775758747403)
XLA Ops:
  7.2 0.0 copy-start
  7.2 0.0 all-reduce.4.cloned.1.call-start
  7.2 1.3 copy-done
  8.5 0.0 copy-start.4
  8.5 0.0 copy-start.5
  8.5 6.6 multiply_convert_fusion.1
  15.1 0.0 copy-start.1
  15.1 0.0 copy-start.3
  15.1 2.4 copy-done.1
  17.4 0.0 copy-done.4
  17.4 0.0 copy-done.5
  17.5 0.0 copy-start.2
  17.5 1.5 fusion.39
  18.9 0.0 copy-start.7
  18.9 25.8 %all_gather.3 = bf16[40,4,512]{2,1,0:T(4,128)(2,1)S(1)} all-gather(bf16[5,4,512]{2,1,0:T(4,128)(2,1)S(1)} %get-tuple-element.35), channel_id=1, replica_groups=mesh['mem'=8,'lat'=32,'rep'=2] {'mem'}, dimensions={0}, use_global_device_ids=true | all-gather | bytes 184320 | tf_op jit(solution)/shard_map/all_gather | solution.py:32
  44.7 1.1 copy.29
  45.8 0.0 copy-done.3
  45.8 0.2 multiply_reduce_fusion
  46.0 0.0 copy-done.2
  46.0 0.4 fusion.16
  46.4 0.1 fusion.14
  46.6 0.1 iota_compare_fusion.3
  46.7 143.5 %all-reduce.1 = (f32[5,40,8]{1,2,0:T(8,128)S(1)}, f32[5,8]{1,0:T(8,128)S(1)}) all-reduce(f32[5,40,8]{1,2,0:T(8,128)S(1)} %fusion.16, f32[5,8]{1,0:T(8,128)S(1)} %fusion.14), channel_id=1, replica_groups=mesh['mem'=8,'lat'=32,'rep'=2] {'lat'}, use_global_device_ids=true, to_apply=%region_3.4 | all-reduce | flops 1640 | bytes 13120 | tf_op jit(solution)/shard_map/psum | solution.py:36
  190.2 1.1 fusion.40
  191.3 1.8 copy.30
  193.1 3.8 fusion.41
  196.9 1.6 copy.31
  198.5 0.1 fusion.13
  198.6 0.2 convert_reduce_fusion.1
  198.8 0.0 copy-done.7
  198.8 7.2 convert_reduce_fusion
  206.0 0.0 copy-start.8
  206.0 2.3 copy-done.8
  208.3 2.5 convolution_bitcast_fusion
  210.9 0.0 copy-start.6
  210.9 0.0 all-reduce.4.cloned.1.call-update
  210.9 3.3 convolution_bitcast_fusion.1
  214.2 1363.8 %all-reduce = (f32[4,1024]{1,0:T(4,128)S(1)}, f32[1024]{0:T(1024)S(1)}, f32[4]{0:T(128)S(1)}) all-reduce(f32[4,1024]{1,0:T(4,128)S(1)} %convolution_bitcast_fusion.1, f32[1024]{0:T(1024)S(1)} %get-tuple-element.38, f32[4]{0:T(128)S(1)} %get-tuple-element.30), channel_id=1, replica_groups=mesh['mem'=8,'lat'=32,'rep'=2] {'mem','lat'}, use_global_device_ids=true, to_apply=%region_6.7 | all-reduce | flops 5124 | bytes 40992 | tf_op jit(solution)/shard_map/psum | solution.py:61
  1578.0 0.5 broadcast_multiply_fusion.3
  1578.5 0.6 broadcast_multiply_fusion.2
  1579.1 0.6 broadcast_multiply_fusion.1
  1579.7 0.0 copy-done.6
  1579.7 5.1 convolution_convert_fusion
  1584.8 0.0 all-reduce.4.cloned.1.call-done
  1584.8 1.3 broadcast_multiply_fusion
  1586.2 1.3 copy.33
  (3 shorter events, 0.1 us)
Async XLA Ops:
  7.2 1.3 copy-start
  7.2 1577.7 %all-reduce.4.cloned.1.call-start = ((), (), s32[]{:S(2)}) async-start(), calls=%async_computation | async-start | bytes 2097152 | tf_op jit(solution)/shard_map/psum | solution.py:61
  8.5 9.0 copy-start.4
  8.5 9.0 copy-start.5
  15.1 2.4 copy-start.1
  15.1 30.7 %copy-start.3 = (f32[4,512]{1,0:T(4,128)S(1)}, f32[4,512]{1,0:T(4,128)}, u32[]{:S(2)}) copy-start(f32[4,512]{1,0:T(4,128)} %param.12) | copy-start | bytes 24580
  17.5 28.6 %copy-start.2 = (s32[512]{0:T(512)S(1)}, s32[512]{0:T(512)}, u32[]{:S(2)}) copy-start(s32[512]{0:T(512)} %param.13) | copy-start | bytes 6148
  18.9 179.9 %copy-start.7 = (f32[1024]{0:T(1024)S(1)}, f32[1024]{0:T(1024)}, u32[]{:S(2)}) copy-start(f32[1024]{0:T(1024)} %param.9) | copy-start | bytes 12292
  206.0 2.3 copy-start.8
  210.9 1368.8 %copy-start.6 = (bf16[256,1024]{1,0:T(8,128)(2,1)S(1)}, bf16[256,1024]{1,0:T(8,128)(2,1)}, u32[]{:S(2)}) copy-start(bf16[256,1024]{1,0:T(8,128)(2,1)} %param.8) | copy-start | bytes 1572868
Sparse Core Ops, SparseCore 0:
  211.0 232.3 all-reduce.3
where the time goes:
time: 1590 us
  blocking collectives  1530 us (96%)
  matrix products  31.9 us (2%)
    psum x1, blocking collectives, local(): lax.psum((in_part, out_part, bin_part, bout_part), ('mem', 'lat'))  1360 us
    psum x1, blocking collectives, local(): pair_sum, obs_sum = lax.psum((pair_part, obs_part), 'lat')  144 us
  transfers between devices with their start and end apart: 1, of which 0 were waited for; matrix products, arithmetic and copies ran while one was open for 1% of the time, Pallas kernels for 0%

commit v1 on v0

v1 whole, which is shorter than its diff:
```python
import jax
import jax.numpy as jnp
from jax import lax
from jax.sharding import Mesh
from jax.sharding import PartitionSpec as P

epsilon = 1e-06
LAT = ("band", "yl", "x")
GROUP = ("yl", "x")


def gather(block, axes, count):
    return lax.all_to_all(jnp.broadcast_to(block[None], (count, *block.shape)), axes, 0, 0)


def local(latent, in_weight, in_bias, out_weight, out_bias, observed, patch_of_cell):
    members_here, cells_here, width = latent.shape
    hid = in_weight.shape[1]
    n_mem = lax.axis_size("mem")
    n_lat = lax.axis_size(LAT)
    n_group = lax.axis_size(GROUP)
    members = members_here * n_mem
    nvars = out_weight.shape[0]
    entries = float(nvars * 4 * cells_here)
    highest = lax.Precision.HIGHEST
    preact = (
        jnp.einsum("mcd,dk->mck", latent, in_weight, preferred_element_type=jnp.float32) + in_bias
    )
    hidden = jax.nn.silu(preact).astype(jnp.bfloat16)
    field = (
        jnp.einsum("mck,vk->mvc", hidden, out_weight, preferred_element_type=jnp.float32)
        + out_bias[None, :, None]
    ).astype(jnp.bfloat16)
    own_patch = patch_of_cell - 2 * lax.axis_index("band")
    in_patch = (own_patch[:, None] == jnp.arange(2, dtype=jnp.int32)[None, :]).astype(jnp.float32)
    own_field = field.astype(jnp.float32)
    misfit = own_field - observed[None]
    obs_part = jnp.dot(jnp.sum(misfit * misfit, axis=1), in_patch, precision=highest)
    all_fields = gather(field.reshape(members_here * nvars, cells_here), "mem", n_mem)
    all_fields = all_fields.reshape(members, nvars, cells_here)
    diff = own_field[:, None] - all_fields.astype(jnp.float32)[None]
    squared = jnp.sum(diff * diff, axis=2)
    pair_part = jnp.einsum("mnc,cp->mnp", squared, in_patch, precision=highest)
    flat = jnp.concatenate([pair_part.reshape(-1), obs_part.reshape(-1)])
    room = -(-flat.size // 1024) * 1024
    flat = jnp.pad(flat, (0, room - flat.size)).reshape(-1, 128)
    sums = jnp.sum(gather(flat, GROUP, n_group), axis=0).reshape(-1)
    pair_sum = sums[: members_here * members * 2].reshape(members_here, members, 2)
    obs_sum = sums[members_here * members * 2 :][: members_here * 2].reshape(members_here, 2)
    spread = jnp.sqrt(obs_sum / entries + epsilon)
    dist = jnp.sqrt(pair_sum / entries + epsilon)
    own_ids = lax.axis_index("mem") * members_here + jnp.arange(members_here, dtype=jnp.int32)
    other_ids = jnp.arange(members, dtype=jnp.int32)
    inv_dist = jnp.where(
        (own_ids[:, None] != other_ids[None, :])[:, :, None], 1.0 / dist, jnp.float32(0.0)
    )
    first = (own_patch == 0)[None, None, :]
    cell_w = jnp.where(first, inv_dist[:, :, :1], inv_dist[:, :, 1:])
    cell_spread = jnp.where(first[0], spread[:, :1], spread[:, 1:])
    pulled = jnp.sum(cell_w[:, :, None, :] * diff, axis=1)
    grad_field = (misfit / cell_spread[:, None, :] - pulled / members).astype(jnp.bfloat16)
    d_hidden = jnp.einsum("mvc,vk->mck", grad_field, out_weight, preferred_element_type=jnp.float32)
    gate_sig = jax.nn.sigmoid(preact)
    d_preact = (d_hidden * gate_sig * (1.0 + preact * (1.0 - gate_sig))).astype(jnp.bfloat16)
    d_latent = jnp.einsum(
        "mck,dk->mcd", d_preact, in_weight, preferred_element_type=jnp.float32
    ).astype(jnp.bfloat16)
    out_part = jnp.einsum("mvc,mck->vk", grad_field, hidden, preferred_element_type=jnp.float32)
    bin_part = jnp.sum(d_preact, axis=(0, 1), dtype=jnp.float32)
    bout_part = jnp.sum(grad_field, axis=(0, 2), dtype=jnp.float32)
    in_part = jnp.einsum("mcd,mck->dk", latent, d_preact, preferred_element_type=jnp.float32)
    small = jnp.concatenate(
        [out_part.reshape(-1, 128), bin_part.reshape(-1, 128), jnp.pad(bout_part, (0, 128 - nvars))[None]]
    )
    small = jnp.pad(small, ((0, width - small.shape[0]), (0, 0)))
    rows = width // n_lat
    payload = jnp.concatenate([in_part, small], axis=1).reshape(n_lat, rows, hid + 128)
    share = jnp.sum(lax.all_to_all(payload, LAT, 0, 0), axis=0)
    share = jnp.sum(gather(share, "mem", n_mem), axis=0)
    scale = 1.0 / jnp.sqrt(jnp.float32(members * cells_here * n_lat))
    share = share * scale
    high = share.astype(jnp.bfloat16)
    low = (share[:, hid:] - high[:, hid:].astype(jnp.float32)).astype(jnp.bfloat16)
    whole = gather(jnp.concatenate([high, low], axis=1), LAT, n_lat)
    whole = whole.reshape(width, hid + 256).astype(jnp.float32)
    d_in = whole[:, :hid]
    small = whole[:, hid : hid + 128] + whole[:, hid + 128 :]
    n_out = nvars * hid // 128
    n_bin = hid // 128
    d_out = small[:n_out].reshape(nvars, hid)
    d_bin = small[n_out : n_out + n_bin].reshape(hid)
    d_bout = small[n_out + n_bin, :nvars]
    return (d_latent, d_in, d_out, d_bin, d_bout)


def solution(mesh):
    n_mem, n_lat, n_rep = (mesh.shape[a] for a in ("mem", "lat", "rep"))
    split = Mesh(
        mesh.devices.reshape(n_mem, n_lat // 8, 2, 4, n_rep), ("mem", "band", "yl", "x", "rep")
    )
    placed = (P(("rep", "mem"), LAT, None), P(), P(), P(), P(), P("rep", LAT), P(LAT))
    return jax.shard_map(
        local,
        mesh=split,
        in_specs=placed,
        out_specs=(
            P(("rep", "mem"), LAT, None),
            P("rep", None),
            P("rep", None),
            P("rep"),
            P("rep"),
        ),
        check_vma=False,
    )
```

time: 1590 us -> 142 us (0.09)
  the two profiles are of different devices: /device:TPU:0 before, /device:TPU:8 now
where the time goes in v1:
time: 142 us; the launch traced here: 141 us
  blocking collectives  51 us (36%)
  matrix products  29.6 us (21%)
  waiting for transfers between devices  26.1 us (18%)
  starting transfers between devices  20.9 us (15%)
  local copies, waits for them, and re-layouts  11.4 us (8%)
    all_to_all x1, blocking collectives, local(): share = jnp.sum(lax.all_to_all(payload, LAT, 0, 0), axis=0)  37 us
    all_to_all x3, waiting for transfers between devices, gather(): lax.all_to_all(jnp.broadcast_to(block[None], (count, *block.shape)), axes...  26.1 us
    all_to_all x3, starting transfers between devices, gather(): lax.all_to_all(jnp.broadcast_to(block[None], (count, *block.shape)), axes...  20.9 us
    all_to_all x1, blocking collectives, gather(): lax.all_to_all(jnp.broadcast_to(block[None], (count, *block.shape)), axes...  14 us
    dot_general x1, matrix products, local(): jnp.einsum('mvc,vk->mck', grad_field, out_weight, preferred_element_type=...  8.7 us
    dot_general x1, matrix products, local(): jnp.einsum('mcd,dk->mck', latent, in_weight, preferred_element_type=jnp.f...  6.56 us
    dot_general x1, matrix products, local(): jnp.einsum('mck,dk->mcd', d_preact, in_weight, preferred_element_type=jnp...  5.11 us
    dot_general x1, matrix products, local(): jnp.einsum('mcd,mck->dk', latent, d_preact, preferred_element_type=jnp.fl...  4.03 us
  transfers between devices with their start and end apart: 3, of which 3 were waited for; matrix products, arithmetic and copies ran while one was open for 4% of the time, Pallas kernels for 0%

profile of v1, /device:TPU:8, one launch (start us, length us, event | category | flops | bytes accessed | tf_op | source)
XLA Modules:
  0.0 141.2 jit_solution(3979957803774292256)
XLA Ops:
  0.6 0.0 copy-start
  0.6 0.0 copy-start.3
  0.7 0.0 copy-start.4
  0.7 0.0 copy-start.2
  0.7 1.3 copy-done
  2.0 6.6 %multiply_convert_fusion.1 = (bf16[5,512,1024]{2,1,0:T(8,128)(2,1)S(1)}, f32[5,512,1024]{2,1,0:T(8,128)}) fusion(f32[1024]{0:T(1024)} %param.9, bf16[5,512,256]{2,1,0:T(8,128)(2,1)S(1)} %copy-done, bf16[256,1024]{1,0:T(8,128)(2,1)} %param.8), kind=kOutput, calls=%fused_computation.2 | convolution fusion | flops 1357905920 | bytes 17567744 | tf_op jit(solution)/shard_map/mcd,dk->mck/dot_general | solution.py:27
  8.5 0.0 copy-start.1
  8.5 0.0 copy-start.5
  8.5 2.4 %copy-done.1 = bf16[5,512,1024]{2,1,0:T(8,128)(2,1)} copy-done((bf16[5,512,1024]{2,1,0:T(8,128)(2,1)}, bf16[5,512,1024]{2,1,0:T(8,128)(2,1)S(1)}, u32[]{:S(2)}) %copy-start.1) | copy-done | bytes 5242904
  10.9 0.0 copy-done.3
  10.9 0.0 copy-done.4
  10.9 0.0 copy-done.2
  10.9 1.5 %multiply_reduce_fusion = (f32[5,512]{1,0:T(8,128)S(1)}, bf16[5,4,512]{2,1,0:T(4,128)(2,1)S(1)}) fusion(f32[4,512]{1,0:T(4,128)S(1)} %copy-done.2, f32[4]{0:T(128)S(1)} %copy-done.4, bf16[5,512,1024]{2,1,0:T(8,128)(2,1)S(1)} %get-tuple-element.15, bf16[4,1024]{1,0:T(4,128)(2,1)S(1)} %copy-done.3), kind=kOutput, calls=%fused_computation.27 | convolution fusion | flops 21030400 | bytes 5290000 | tf_op jit(solution)/shard_map/mck,vk->mvc/dot_general | solution.py:31
  12.4 0.7 broadcast_in_dim.112
  13.1 10.3 %all-to-all-start = ((bf16[8,20,512]{2,1,0:T(8,128)(2,1)}), bf16[8,20,512]{2,1,0:T(8,128)(2,1)S(1)}, u32[]{:S(2)}, u32[]{:S(2)}) async-start(bf16[8,20,512]{2,1,0:T(8,128)(2,1)} %broadcast_in_dim.112), calls=%async_computation | async-start | bytes 393216 | tf_op jit(solution)/shard_map/all_to_all | solution.py:13
  23.4 0.0 copy-done.5
  23.4 0.1 fusion.16
  23.6 0.1 reshape.126
  23.6 10.2 %all-to-all-done = bf16[8,20,512]{2,1,0:T(8,128)(2,1)S(1)} async-done(((bf16[8,20,512]{2,1,0:T(8,128)(2,1)}), bf16[8,20,512]{2,1,0:T(8,128)(2,1)S(1)}, u32[]{:S(2)}, u32[]{:S(2)}) %all-to-all-start) | async-done | bytes 163872 | tf_op jit(solution)/shard_map/all_to_all | solution.py:13
  33.9 0.1 reshape.133
  34.0 0.1 copy.34
  34.1 0.2 fusion
  34.3 0.3 fusion.10
  34.6 0.1 reshape.125
  34.8 0.1 fusion.15
  34.8 0.6 broadcast_in_dim.114
  35.5 5.8 %all-to-all-start.1 = ((f32[8,8,128]{2,1,0:T(8,128)}), f32[8,8,128]{2,1,0:T(8,128)S(1)}, u32[]{:S(2)}, u32[]{:S(2)}) async-start(f32[8,8,128]{2,1,0:T(8,128)} %broadcast_in_dim.114), calls=%async_computation.1 | async-start | bytes 65536 | tf_op jit(solution)/shard_map/all_to_all | solution.py:13
  41.2 0.1 iota_compare_fusion.2
  41.3 4.8 %all-to-all-done.1 = f32[8,8,128]{2,1,0:T(8,128)S(1)} async-done(((f32[8,8,128]{2,1,0:T(8,128)}), f32[8,8,128]{2,1,0:T(8,128)S(1)}, u32[]{:S(2)}, u32[]{:S(2)}) %all-to-all-start.1) | async-done | bytes 32800 | tf_op jit(solution)/shard_map/all_to_all | solution.py:13
  46.1 0.2 slice.47
  46.3 0.0 copy-start.7
  46.3 0.1 sqrt.10
  46.5 0.1 broadcast_select_fusion.1
  46.6 0.2 slice_reduce_fusion.1
  46.7 0.1 broadcast_select_fusion
  46.9 0.3 fusion.1
  47.1 0.2 slice_reduce_fusion.3
  47.3 0.1 broadcast_select_fusion.2
  47.4 0.2 convert_reduce_fusion.1
  47.5 3.3 %convolution_bitcast_fusion.1 = f32[4,1024]{1,0:T(4,128)S(1)} fusion(bf16[5,4,512]{2,1,0:T(4,128)(2,1)S(1)} %get-tuple-element.10, bf16[5,512,1024]{2,1,0:T(8,128)(2,1)} %copy-done.1), kind=kOutput, calls=%fused_computation.15 | convolution fusion | flops 20971520 | bytes 5279744 | tf_op jit(solution)/shard_map/mvc,mck->vk/dot_general | solution.py:68
  50.8 0.0 copy-done.7
  50.8 8.7 %convert_reduce_fusion = (f32[1024]{0:T(1024)S(1)}, bf16[5,512,1024]{2,1,0:T(8,128)(2,1)}) fusion(f32[5,512,1024]{2,1,0:T(8,128)} %get-tuple-element.16, f32[1024]{0:T(1024)S(1)} %copy-done.7, bf16[5,4,512]{2,1,0:T(4,128)(2,1)S(1)} %get-tuple-element.10, bf16[4,1024]{1,0:T(4,128)(2,1)S(1)} %copy-done.3), kind=kOutput, calls=%fused_computation | convolution fusion | flops 52427776 | bytes 15765504 | tf_op jit(solution)/shard_map/mvc,vk->mck/dot_general | solution.py:62
  59.6 0.1 copy.38
  59.7 4.0 %convolution_bitcast_fusion = f32[256,1024]{0,1:T(8,128)S(1)} fusion(bf16[5,512,1024]{2,1,0:T(8,128)(2,1)} %get-tuple-element.20, bf16[5,512,256]{2,1,0:T(8,128)(2,1)S(1)} %copy-done), kind=kOutput, calls=%fused_computation.9 | convolution fusion | flops 1342177280 | bytes 7602176 | tf_op jit(solution)/shard_map/mcd,mck->dk/dot_general | solution.py:71
  63.7 0.0 copy-start.6
  63.7 0.1 select_maximum_fusion
  63.8 1.4 copy.39
  65.2 37.0 %all_to_all.25 = f32[32,8,1152]{2,1,0:T(8,128)S(1)} all-to-all(f32[32,8,1152]{2,1,0:T(8,128)} %bitcast.51), channel_id=1, replica_groups=mesh['mem'=8,'band'=4,'yl'=2,'x'=4,'rep'=2] {'band','yl','x'}, dimensions={0} | all-to-all | bytes 2359296 | tf_op jit(solution)/shard_map/all_to_all | solution.py:78
  102.2 0.1 reduce_sum.78
  102.3 14.0 %all_to_all.26 = f32[8,8,1152]{2,1,0:T(8,128)S(1)} all-to-all(f32[8,8,1152]{2,1,0:T(8,128)S(1)} %broadcast_in_dim.127), channel_id=1, replica_groups=mesh['mem'=8,'band'=4,'yl'=2,'x'=4,'rep'=2] {'mem'}, dimensions={0} | all-to-all | bytes 589824 | tf_op jit(solution)/shard_map/all_to_all | solution.py:13
  116.4 0.9 broadcast_in_dim.128
  117.2 4.8 %all-to-all-start.4 = ((bf16[32,8,1280]{2,1,0:T(8,128)(2,1)}), bf16[32,8,1280]{2,1,0:T(8,128)(2,1)S(1)}, u32[]{:S(2)}, u32[]{:S(2)}) async-start(bf16[32,8,1280]{2,1,0:T(8,128)(2,1)} %broadcast_in_dim.128), calls=%async_computation.4 | async-start | bytes 1310720 | tf_op jit(solution)/shard_map/all_to_all | solution.py:13
  122.0 0.0 copy-done.6
  122.0 5.1 %convolution_convert_fusion = bf16[5,512,256]{2,1,0:T(8,128)(2,1)} fusion(bf16[5,512,1024]{2,1,0:T(8,128)(2,1)} %get-tuple-element.20, bf16[256,1024]{1,0:T(8,128)(2,1)S(1)} %copy-done.6), kind=kOutput, calls=%fused_computation.8 | convolution fusion | flops 1342832640 | bytes 7077888 | tf_op jit(solution)/shard_map/mck,dk->mcd/dot_general | solution.py:65
  127.2 11.1 %all-to-all-done.4 = bf16[32,8,1280]{2,1,0:T(8,128)(2,1)S(1)} async-done(((bf16[32,8,1280]{2,1,0:T(8,128)(2,1)}), bf16[32,8,1280]{2,1,0:T(8,128)(2,1)S(1)}, u32[]{:S(2)}, u32[]{:S(2)}) %all-to-all-start.4) | async-done | bytes 655392 | tf_op jit(solution)/shard_map/all_to_all | solution.py:13
  138.2 0.1 bitcast_convert_fusion
  138.3 1.1 slice.67
  139.4 0.6 slice_bitcast_fusion
  140.0 0.5 slice_bitcast_fusion.1
  140.6 0.6 reshape.131
  (17 shorter events, 0.2 us)
Async XLA Ops:
  0.6 1.3 copy-start
  0.6 10.2 %copy-start.3 = (bf16[4,1024]{1,0:T(4,128)(2,1)S(1)}, bf16[4,1024]{1,0:T(4,128)(2,1)}, u32[]{:S(2)}) copy-start(bf16[4,1024]{1,0:T(4,128)(2,1)} %param.10) | copy-start | bytes 24580
  0.7 10.2 %copy-start.4 = (f32[4]{0:T(128)S(1)}, f32[4]{0:T(128)}, u32[]{:S(2)}) copy-start(f32[4]{0:T(128)} %param.11) | copy-start | bytes 52
  0.7 10.2 %copy-start.2 = (f32[4,512]{1,0:T(4,128)S(1)}, f32[4,512]{1,0:T(4,128)}, u32[]{:S(2)}) copy-start(f32[4,512]{1,0:T(4,128)} %param.12) | copy-start | bytes 24580
  8.5 2.4 %copy-start.1 = (bf16[5,512,1024]{2,1,0:T(8,128)(2,1)}, bf16[5,512,1024]{2,1,0:T(8,128)(2,1)S(1)}, u32[]{:S(2)}) copy-start(bf16[5,512,1024]{2,1,0:T(8,128)(2,1)S(1)} %get-tuple-element.15) | copy-start | bytes 15728644
  8.5 14.9 %copy-start.5 = (s32[512]{0:T(512)S(1)}, s32[512]{0:T(512)}, u32[]{:S(2)}) copy-start(s32[512]{0:T(512)} %param.13) | copy-start | bytes 6148
  13.1 20.8 %all-to-all-start = ((bf16[8,20,512]{2,1,0:T(8,128)(2,1)}), bf16[8,20,512]{2,1,0:T(8,128)(2,1)S(1)}, u32[]{:S(2)}, u32[]{:S(2)}) async-start(bf16[8,20,512]{2,1,0:T(8,128)(2,1)} %broadcast_in_dim.112), calls=%async_computation | async-start | bytes 393216 | tf_op jit(solution)/shard_map/all_to_all | solution.py:13
  35.5 10.6 %all-to-all-start.1 = ((f32[8,8,128]{2,1,0:T(8,128)}), f32[8,8,128]{2,1,0:T(8,128)S(1)}, u32[]{:S(2)}, u32[]{:S(2)}) async-start(f32[8,8,128]{2,1,0:T(8,128)} %broadcast_in_dim.114), calls=%async_computation.1 | async-start | bytes 65536 | tf_op jit(solution)/shard_map/all_to_all | solution.py:13
  46.3 4.6 %copy-start.7 = (f32[1024]{0:T(1024)S(1)}, f32[1024]{0:T(1024)}, u32[]{:S(2)}) copy-start(f32[1024]{0:T(1024)} %param.9) | copy-start | bytes 12292
  63.7 58.3 %copy-start.6 = (bf16[256,1024]{1,0:T(8,128)(2,1)S(1)}, bf16[256,1024]{1,0:T(8,128)(2,1)}, u32[]{:S(2)}) copy-start(bf16[256,1024]{1,0:T(8,128)(2,1)} %param.8) | copy-start | bytes 1572868
  117.2 21.0 %all-to-all-start.4 = ((bf16[32,8,1280]{2,1,0:T(8,128)(2,1)}), bf16[32,8,1280]{2,1,0:T(8,128)(2,1)S(1)}, u32[]{:S(2)}, u32[]{:S(2)}) async-start(bf16[32,8,1280]{2,1,0:T(8,128)(2,1)} %broadcast_in_dim.128), calls=%async_computation.4 | async-start | bytes 1310720 | tf_op jit(solution)/shard_map/all_to_all | solution.py:13

commit v2 on v1

v2 whole, which is shorter than its diff:
```python
import functools

import jax
import jax.numpy as jnp
from jax import lax
from jax.experimental import pallas as pl
from jax.experimental.pallas import tpu as pltpu
from jax.sharding import Mesh
from jax.sharding import PartitionSpec as P

epsilon = 1e-06
LAT = ("band", "yl", "x")
GROUP = ("yl", "x")
f32, bf16 = jnp.float32, jnp.bfloat16
NN = (((1,), (0,)), ((), ()))
NT = (((1,), (1,)), ((), ()))
TN = (((0,), (0,)), ((), ()))
LANES = 128
TAIL = 8
PARAMS = pltpu.CompilerParams(vmem_limit_bytes=48 * 2**20)


def dot(a, b, dims):
    return lax.dot_general(a, b, dims, preferred_element_type=f32)


def exchange(blocks, axes):
    return lax.all_to_all(blocks, axes, 0, 0)


def quantize(block):
    top = jnp.max(jnp.abs(block), keepdims=True)
    exponent = jnp.clip(jnp.ceil(jnp.log2(jnp.maximum(top, 1e-33))), -110.0, 110.0)
    whole = jnp.clip(jnp.round(block * jnp.exp2(15.0 - exponent)), -32767.0, 32767.0)
    return whole.astype(jnp.int32), exponent.astype(jnp.int32)


def encode(block, tail):
    row = lax.broadcasted_iota(jnp.int32, tail.shape, 0)
    codes, exponent = quantize(block)
    tail_codes, tail_exponent = quantize(jnp.where(row < TAIL - 2, tail, 0.0))
    last = jnp.where(
        row == TAIL - 2, exponent, jnp.where(row == TAIL - 1, tail_exponent, tail_codes)
    )
    return jnp.concatenate([codes, last], axis=0).astype(jnp.int16)


def decode(chunk):
    values = chunk.astype(jnp.int32).astype(f32)
    rows = values.shape[0] - TAIL
    block = values[:rows] * jnp.exp2(values[rows + TAIL - 2 : rows + TAIL - 1] - 15.0)
    tail = values[rows:] * jnp.exp2(values[rows + TAIL - 1 :] - 15.0)
    row = lax.broadcasted_iota(jnp.int32, tail.shape, 0)
    return block, jnp.where(row < TAIL - 2, tail, 0.0)


def forward_kernel(n_blocks, x_ref, w_ref, b_ref, wo_ref, bo_ref, f_ref):
    x = x_ref[0]
    step = w_ref.shape[1] // n_blocks
    total = bo_ref[...]
    for k in range(n_blocks):
        cols = slice(k * step, (k + 1) * step)
        half = 0.5 * (dot(x, w_ref[:, cols], NN) + b_ref[:, cols])
        hidden = (half * jnp.tanh(half) + half).astype(bf16)
        total = total + dot(wo_ref[:, cols], hidden, NT)
    field = total.astype(bf16)
    for copy in range(f_ref.shape[0]):
        f_ref[copy, pl.program_id(0)] = field


def forward(latent, w, b, wo, bo, copies):
    members, cells, width = latent.shape
    nvars, hid = wo.shape
    const = lambda i: (0, 0)
    return pl.pallas_call(
        functools.partial(forward_kernel, 8),
        grid=(members,),
        in_specs=[
            pl.BlockSpec((1, cells, width), lambda i: (i, 0, 0)),
            pl.BlockSpec((width, hid), const),
            pl.BlockSpec((1, hid), const),
            pl.BlockSpec((nvars, hid), const),
            pl.BlockSpec((nvars, 1), const),
        ],
        out_specs=pl.BlockSpec((copies, members, nvars, cells), lambda i: (0, 0, 0, 0)),
        out_shape=jax.ShapeDtypeStruct((copies, members, nvars, cells), bf16),
        compiler_params=PARAMS,
        name="field",
    )(latent, w, b.reshape(1, hid), wo, bo.reshape(nvars, 1))


def backward_kernel(n_blocks, x_ref, w_ref, b_ref, wo_ref, g_ref, dp_ref, pay_ref, acc, small):
    member = pl.program_id(0)

    @pl.when(member == 0)
    def _():
        acc[...] = jnp.zeros_like(acc)
        small[...] = jnp.zeros_like(small)

    x = x_ref[0]
    g = g_ref[0]
    nvars = g.shape[0]
    step = w_ref.shape[1] // n_blocks
    ones = jnp.ones((8, x.shape[0]), bf16)
    for k in range(n_blocks):
        cols = slice(k * step, (k + 1) * step)
        pre = dot(x, w_ref[:, cols], NN) + b_ref[:, cols]
        sig = 0.5 * jnp.tanh(0.5 * pre) + 0.5
        act = pre * sig
        slope = act * (1.0 - sig) + sig
        dp = (dot(g, wo_ref[:, cols], TN) * slope).astype(bf16)
        dp_ref[0, :, cols] = dp
        acc[:, cols] += dot(x, dp, TN)
        small[0:nvars, cols] += dot(g, act.astype(bf16), NN)
        small[nvars : nvars + 1, cols] += dot(ones, dp, NN)[0:1]
    bias = jnp.sum(g.astype(f32), axis=1, keepdims=True)
    for v in range(nvars):
        small[nvars + 1 : nvars + 2, v * LANES : (v + 1) * LANES] += jnp.broadcast_to(
            bias[v : v + 1], (1, LANES)
        )

    @pl.when(member == pl.num_programs(0) - 1)
    def _():
        n_col = acc.shape[1] // LANES
        rows = acc.shape[0] // (pay_ref.shape[0] // n_col)
        owned = [(0, nvars), (nvars, nvars + 1), (nvars + 1, nvars + 2), (0, 0)]
        for rb, (low, high) in enumerate(owned):
            for cb in range(n_col):
                lanes = slice(cb * LANES, (cb + 1) * LANES)
                row = lax.broadcasted_iota(jnp.int32, (TAIL, LANES), 0)
                tail = jnp.where((row >= low) & (row < high), small[:, lanes], 0.0)
                pay_ref[rb * n_col + cb] = encode(acc[rb * rows : (rb + 1) * rows, lanes], tail)


def backward(latent, w, b, wo, g, chunks):
    members, cells, width = latent.shape
    nvars, hid = wo.shape
    const = lambda i: (0, 0)
    chunk = (width * hid // (chunks * LANES) + TAIL, LANES)
    return pl.pallas_call(
        functools.partial(backward_kernel, 8),
        grid=(members,),
        in_specs=[
            pl.BlockSpec((1, cells, width), lambda i: (i, 0, 0)),
            pl.BlockSpec((width, hid), const),
            pl.BlockSpec((1, hid), const),
            pl.BlockSpec((nvars, hid), const),
            pl.BlockSpec((1, nvars, cells), lambda i: (i, 0, 0)),
        ],
        out_specs=[
            pl.BlockSpec((1, cells, hid), lambda i: (i, 0, 0)),
            pl.BlockSpec((chunks, *chunk), lambda i: (0, 0, 0)),
        ],
        out_shape=[
            jax.ShapeDtypeStruct((members, cells, hid), bf16),
            jax.ShapeDtypeStruct((chunks, *chunk), jnp.int16),
        ],
        scratch_shapes=[pltpu.VMEM((width, hid), f32), pltpu.VMEM((TAIL, hid), f32)],
        compiler_params=PARAMS,
        name="backward",
    )(latent, w, b.reshape(1, hid), wo, g)


def down_kernel(dp_ref, w_ref, o_ref):
    o_ref[0] = dot(dp_ref[0], w_ref[...], NT).astype(bf16)


def down(dp, w):
    members, cells, hid = dp.shape
    width = w.shape[0]
    return pl.pallas_call(
        down_kernel,
        grid=(members,),
        in_specs=[
            pl.BlockSpec((1, cells, hid), lambda i: (i, 0, 0)),
            pl.BlockSpec((width, hid), lambda i: (0, 0)),
        ],
        out_specs=pl.BlockSpec((1, cells, width), lambda i: (i, 0, 0)),
        out_shape=jax.ShapeDtypeStruct((members, cells, width), bf16),
        compiler_params=PARAMS,
        name="d_latent",
    )(dp, w)


def reduce_kernel(scale, in_ref, out_ref):
    total, tail = decode(in_ref[0])
    for source in range(1, in_ref.shape[0]):
        block, more = decode(in_ref[source])
        total, tail = total + block, tail + more
    chunk = encode(total * scale, tail * scale)
    for copy in range(out_ref.shape[0]):
        out_ref[copy] = chunk


def reduce_and_copy(received, copies, scale, name):
    return pl.pallas_call(
        functools.partial(reduce_kernel, scale),
        out_shape=jax.ShapeDtypeStruct((copies, *received.shape[1:]), jnp.int16),
        compiler_params=PARAMS,
        name=name,
    )(received)


def spread_kernel(in_ref, d_in_ref, small_ref):
    n_col = d_in_ref.shape[1] // LANES
    rows = in_ref.shape[1] - TAIL
    for cb in range(n_col):
        lanes = slice(cb * LANES, (cb + 1) * LANES)
        tails = None
        for rb in range(in_ref.shape[0] // n_col):
            block, tail = decode(in_ref[rb * n_col + cb])
            d_in_ref[rb * rows : (rb + 1) * rows, lanes] = block
            tails = tail if tails is None else tails + tail
        small_ref[:, lanes] = tails


def spread_out(received, width, hid):
    return pl.pallas_call(
        spread_kernel,
        out_shape=[
            jax.ShapeDtypeStruct((width, hid), f32),
            jax.ShapeDtypeStruct((TAIL, hid), f32),
        ],
        compiler_params=PARAMS,
        name="outputs",
    )(received)


def local(latent, in_weight, in_bias, out_weight, out_bias, observed, patch_of_cell):
    members_here, cells_here, width = latent.shape
    nvars, hid = out_weight.shape
    n_mem = lax.axis_size("mem")
    n_lat = lax.axis_size(LAT)
    n_group = lax.axis_size(GROUP)
    members = members_here * n_mem
    entries = float(nvars * 4 * cells_here)
    highest = lax.Precision.HIGHEST
    copies = forward(latent, in_weight, in_bias, out_weight, out_bias, n_mem)
    all_fields = exchange(copies, "mem").reshape(members, nvars, cells_here).astype(f32)
    own_field = copies[0].astype(f32)
    own_patch = patch_of_cell - 2 * lax.axis_index("band")
    in_patch = (own_patch[:, None] == jnp.arange(2, dtype=jnp.int32)[None, :]).astype(f32)
    misfit = own_field - observed[None]
    obs_part = jnp.dot(jnp.sum(misfit * misfit, axis=1), in_patch, precision=highest)
    diff = own_field[:, None] - all_fields[None]
    squared = jnp.sum(diff * diff, axis=2)
    pair_part = jnp.einsum("mnc,cp->mnp", squared, in_patch, precision=highest)
    flat = jnp.concatenate([pair_part.reshape(-1), obs_part.reshape(-1)])
    room = -(-flat.size // 1024) * 1024
    flat = jnp.pad(flat, (0, room - flat.size)).reshape(-1, 128)
    sums = exchange(jnp.broadcast_to(flat[None], (n_group, *flat.shape)), GROUP)
    sums = jnp.sum(sums, axis=0).reshape(-1)
    pair_sum = sums[: members_here * members * 2].reshape(members_here, members, 2)
    obs_sum = sums[members_here * members * 2 :][: members_here * 2].reshape(members_here, 2)
    spread = jnp.sqrt(obs_sum / entries + epsilon)
    dist = jnp.sqrt(pair_sum / entries + epsilon)
    own_ids = lax.axis_index("mem") * members_here + jnp.arange(members_here, dtype=jnp.int32)
    other_ids = jnp.arange(members, dtype=jnp.int32)
    inv_dist = jnp.where(
        (own_ids[:, None] != other_ids[None, :])[:, :, None], 1.0 / dist, jnp.float32(0.0)
    )
    first = (own_patch == 0)[None, None, :]
    cell_w = jnp.where(first, inv_dist[:, :, :1], inv_dist[:, :, 1:])
    cell_spread = jnp.where(first[0], spread[:, :1], spread[:, 1:])
    pulled = jnp.sum(cell_w[:, :, None, :] * diff, axis=1)
    grad_field = (misfit / cell_spread[:, None, :] - pulled / members).astype(bf16)
    d_preact, payload = backward(latent, in_weight, in_bias, out_weight, grad_field, n_lat)
    d_latent = down(d_preact, in_weight)
    scale = 1.0 / (members * cells_here * n_lat) ** 0.5
    payload = reduce_and_copy(exchange(payload, LAT), n_mem, 1.0, "lat_sum")
    payload = reduce_and_copy(exchange(payload, "mem"), n_lat, scale, "mem_sum")
    d_in, small = spread_out(exchange(payload, LAT), width, hid)
    d_bout = small[nvars + 1].reshape(-1, LANES)[:nvars, 0]
    return (d_latent, d_in, small[:nvars], small[nvars], d_bout)


def solution(mesh):
    n_mem, n_lat, n_rep = (mesh.shape[a] for a in ("mem", "lat", "rep"))
    split = Mesh(
        mesh.devices.reshape(n_mem, n_lat // 8, 2, 4, n_rep), ("mem", "band", "yl", "x", "rep")
    )
    placed = (P(("rep", "mem"), LAT, None), P(), P(), P(), P(), P("rep", LAT), P(LAT))
    return jax.shard_map(
        local,
        mesh=split,
        in_specs=placed,
        out_specs=(
            P(("rep", "mem"), LAT, None),
            P("rep", None),
            P("rep", None),
            P("rep"),
            P("rep"),
        ),
        check_vma=False,
    )
```

time: 142 us -> 124 us (0.87)
  matrix products: 29.6 us -> 0.43 us
  Pallas kernels: 0 us -> 29 us
  blocking collectives: 51 us -> 35.6 us
  waiting for transfers between devices: 26.1 us -> 22.1 us
  other arithmetic: 1.36 us -> 3.2 us
    dot_general x6 -> x0, matrix products: 29.2 us -> none  [the longest x1 8.7 us: local(): jnp.einsum('mvc,vk->mck', grad_field, out_weight, preferred_element_type=...]
    pallas_call x0 -> x6, Pallas kernels: none -> 29 us  [the longest x1 15.4 us: backward(): pl.pallas_call(functools.partial(backward_kernel, 8), grid=(members,), in...]
    all_to_all x2, blocking collectives: 51 us -> 35.6 us  [exchange(): return lax.all_to_all(blocks, axes, 0, 0)]
    all_to_all x3, waiting for transfers between devices: 26.1 us -> 22.1 us  [exchange(): return lax.all_to_all(blocks, axes, 0, 0)]
    unnamed x16 -> x23, local copies, waits for them, and re-layouts: 3.68 us -> 6.85 us
    broadcast_in_dim x6 -> x1, local copies, waits for them, and re-layouts: 2.24 us -> 0.63 us  [local(): sums = exchange(jnp.broadcast_to(flat[None], (n_group, *flat.shape)), GROUP)]
    concatenate x2 -> x0, local copies, waits for them, and re-layouts: 1.49 us -> none  [the longest x1 1.38 us: local(): jnp.concatenate([in_part, small], axis=1).reshape(n_lat, rows, hid + 128)]
    convert_element_type x4 -> x3, other arithmetic: 0.11 us -> 1.53 us  [the longest x1 0.76 us: local(): (misfit / cell_spread[:, None, :] - pulled / members).astype(bf16)]
  transfers between devices with their start and end apart: 3 -> 3, of which waited for: 3 -> 3; matrix products, arithmetic and copies ran while one was open for 4% -> 1% of each run, Pallas kernels for 0% -> 3%
where the time goes in v2:
time: 124 us; the launch traced here: 123 us
  blocking collectives  35.6 us (29%)
  Pallas kernels  29 us (23%)
  waiting for transfers between devices  22.1 us (18%)
  starting transfers between devices  21.3 us (17%)
  local copies, waits for them, and re-layouts  10.4 us (8%)
  other arithmetic  3.2 us (3%)
    all_to_all x2, blocking collectives, exchange(): return lax.all_to_all(blocks, axes, 0, 0)  35.6 us
    all_to_all x3, waiting for transfers between devices, exchange(): return lax.all_to_all(blocks, axes, 0, 0)  22.1 us
    all_to_all x3, starting transfers between devices, exchange(): return lax.all_to_all(blocks, axes, 0, 0)  21.3 us
    pallas_call x1, Pallas kernels, backward(): pl.pallas_call(functools.partial(backward_kernel, 8), grid=(members,), in...  15.4 us
    pallas_call x1, Pallas kernels, forward(): pl.pallas_call(functools.partial(forward_kernel, 8), grid=(members,), in_...  7.49 us
    unnamed x23, local copies, waits for them, and re-layouts  6.85 us
    pallas_call x1, Pallas kernels, down(): pl.pallas_call(down_kernel, grid=(members,), in_specs=[pl.BlockSpec((1, c...  3.54 us
  transfers between devices with their start and end apart: 3, of which 3 were waited for; matrix products, arithmetic and copies ran while one was open for 1% of the time, Pallas kernels for 3%

profile of v2, /device:TPU:8, one launch (start us, length us, event | category | flops | bytes accessed | tf_op | source)
XLA Modules:
  0.0 122.9 jit_solution(11489582456575281391)
XLA Ops:
  0.6 0.0 copy-start.10
  0.6 0.7 copy.23.bo_ref
  1.4 0.0 copy-start.1
  1.4 1.3 %copy-done.1 = bf16[5,512,256]{2,1,0:T(8,128)(2,1)S(1)} copy-done((bf16[5,512,256]{2,1,0:T(8,128)(2,1)S(1)}, bf16[5,512,256]{2,1,0:T(8,128)(2,1)}, u32[]{:S(2)}) %copy-start.1) | copy-done | bytes 1310744
  2.7 0.0 copy-start.3
  2.7 1.0 copy-done.3
  3.7 0.0 copy-start.5
  3.8 0.7 copy-done.5
  4.4 0.0 copy-start.7
  4.4 0.7 copy-done.7
  5.1 0.0 copy-start.9
  5.1 7.5 %field.1 = bf16[8,5,4,512]{3,2,1,0:T(4,128)(2,1)} custom-call(bf16[5,512,256]{2,1,0:T(8,128)(2,1)S(1)} %copy-done.1, bf16[256,1024]{1,0:T(8,128)(2,1)S(1)} %copy-done.3, f32[1,1024]{1,0:T(1,128)S(1)} %bitcast.25, bf16[4,1024]{1,0:T(4,128)(2,1)S(1)} %copy-done.5, f32[4,1]{1,0:T(4,128)S(1)} %copy.23.bo_ref), custom_call_target="tpu_custom_call" | custom-call | tf_op jit(solution)/shard_map/field/pallas_call | solution.py:75
  12.6 10.3 %all-to-all-start = ((bf16[8,5,4,512]{3,2,1,0:T(4,128)(2,1)}), bf16[8,5,4,512]{3,2,1,0:T(4,128)(2,1)S(1)}, u32[]{:S(2)}, u32[]{:S(2)}) async-start(bf16[8,5,4,512]{3,2,1,0:T(4,128)(2,1)} %field.1), calls=%async_computation | async-start | bytes 327680 | tf_op jit(solution)/shard_map/all_to_all | solution.py:28
  22.9 0.0 copy-done.9
  23.0 0.8 multiply_reduce_fusion
  23.7 0.0 copy-done.10
  23.7 0.1 fusion.9
  23.9 0.1 reshape.118
  24.0 0.7 fusion.3
  24.7 8.0 %all-to-all-done = bf16[8,5,4,512]{3,2,1,0:T(4,128)(2,1)S(1)} async-done(((bf16[8,5,4,512]{3,2,1,0:T(4,128)(2,1)}), bf16[8,5,4,512]{3,2,1,0:T(4,128)(2,1)S(1)}, u32[]{:S(2)}, u32[]{:S(2)}) %all-to-all-start) | async-done | bytes 163872 | tf_op jit(solution)/shard_map/all_to_all | solution.py:28
  32.7 0.1 copy.24
  32.9 0.2 fusion
  33.0 0.0 copy-start.2
  33.1 0.0 copy-start.4
  33.1 0.0 copy-start.6
  33.1 0.0 copy-start.8
  33.1 0.3 fusion.4
  33.4 0.1 reshape.117
  33.6 0.1 fusion.8
  33.6 0.6 broadcast_in_dim.88
  34.3 5.8 %all-to-all-start.1 = ((f32[8,8,128]{2,1,0:T(8,128)}), f32[8,8,128]{2,1,0:T(8,128)S(1)}, u32[]{:S(2)}, u32[]{:S(2)}) async-start(f32[8,8,128]{2,1,0:T(8,128)} %broadcast_in_dim.88), calls=%async_computation.1 | async-start | bytes 65536 | tf_op jit(solution)/shard_map/all_to_all | solution.py:28
  40.0 0.1 iota_compare_fusion.1
  40.1 4.8 %all-to-all-done.1 = f32[8,8,128]{2,1,0:T(8,128)S(1)} async-done(((f32[8,8,128]{2,1,0:T(8,128)}), f32[8,8,128]{2,1,0:T(8,128)S(1)}, u32[]{:S(2)}, u32[]{:S(2)}) %all-to-all-start.1) | async-done | bytes 32800 | tf_op jit(solution)/shard_map/all_to_all | solution.py:28
  44.9 0.2 slice.39
  45.1 0.1 sqrt.10
  45.2 0.1 broadcast_select_fusion.1
  45.3 0.2 slice_reduce_fusion.1
  45.5 0.2 slice_reduce_fusion.3
  45.7 0.1 broadcast_select_fusion
  45.8 0.2 fusion.1
  46.1 0.1 broadcast_select_fusion.2
  46.2 0.8 fusion.2.g_ref
  46.9 0.0 copy-done.2
  46.9 0.0 copy-done.4
  46.9 0.0 copy-done.6
  47.0 0.0 copy-done.8
  47.0 15.4 %backward.1 = (bf16[5,512,1024]{2,1,0:T(8,128)(2,1)}, s16[32,72,128]{2,1,0:T(8,128)(2,1)S(1)}) custom-call(bf16[5,512,256]{2,1,0:T(8,128)(2,1)S(1)} %copy-done.2, bf16[256,1024]{1,0:T(8,128)(2,1)S(1)} %copy-done.4, f32[1,1024]{1,0:T(1,128)S(1)} %bitcast.26, bf16[4,1024]{1,0:T(4,128)(2,1)S(1)} %copy-done.6, bf16[5,4,512]{2,1,0:T(4,128)(2,1)S(1)} %fusion.2.g_ref), custom_call_target="tpu_custom_call" | custom-call | tf_op jit(solution)/shard_map/backward/pallas_call | solution.py:140
  62.4 23.4 %all_to_all.25.in_ref = s16[32,72,128]{2,1,0:T(8,128)(2,1)S(1)} all-to-all(s16[32,72,128]{2,1,0:T(8,128)(2,1)S(1)} %get-tuple-element.10), channel_id=1, replica_groups=mesh['mem'=8,'band'=4,'yl'=2,'x'=4,'rep'=2] {'band','yl','x'}, dimensions={0} | all-to-all | bytes 1179648 | tf_op jit(solution)/shard_map/all_to_all | solution.py:28
  85.8 0.3 lat_sum.1
  86.2 12.2 %all_to_all.26.in_ref = s16[8,72,128]{2,1,0:T(8,128)(2,1)S(1)} all-to-all(s16[8,72,128]{2,1,0:T(8,128)(2,1)S(1)} %lat_sum.1), channel_id=1, replica_groups=mesh['mem'=8,'band'=4,'yl'=2,'x'=4,'rep'=2] {'mem'}, dimensions={0} | all-to-all | bytes 294912 | tf_op jit(solution)/shard_map/all_to_all | solution.py:28
  98.3 1.1 mem_sum.1
  99.4 5.2 %all-to-all-start.4 = ((s16[32,72,128]{2,1,0:T(8,128)(2,1)}), s16[32,72,128]{2,1,0:T(8,128)(2,1)S(1)}, u32[]{:S(2)}, u32[]{:S(2)}) async-start(s16[32,72,128]{2,1,0:T(8,128)(2,1)} %mem_sum.1), calls=%async_computation.4 | async-start | bytes 1179648 | tf_op jit(solution)/shard_map/all_to_all | solution.py:28
  104.7 0.0 copy-start
  104.7 2.5 %copy-done = bf16[5,512,1024]{2,1,0:T(8,128)(2,1)S(1)} copy-done((bf16[5,512,1024]{2,1,0:T(8,128)(2,1)S(1)}, bf16[5,512,1024]{2,1,0:T(8,128)(2,1)}, u32[]{:S(2)}) %copy-start) | copy-done | bytes 5242904
  107.2 3.5 %d_latent.1 = bf16[5,512,256]{2,1,0:T(8,128)(2,1)} custom-call(bf16[5,512,1024]{2,1,0:T(8,128)(2,1)S(1)} %copy-done, bf16[256,1024]{1,0:T(8,128)(2,1)S(1)} %copy-done.4), custom_call_target="tpu_custom_call" | custom-call | tf_op jit(solution)/shard_map/d_latent/pallas_call | solution.py:171
  110.7 9.3 %all-to-all-done.4.in_ref = s16[32,72,128]{2,1,0:T(8,128)(2,1)S(1)} async-done(((s16[32,72,128]{2,1,0:T(8,128)(2,1)}), s16[32,72,128]{2,1,0:T(8,128)(2,1)S(1)}, u32[]{:S(2)}, u32[]{:S(2)}) %all-to-all-start.4) | async-done | bytes 589856 | tf_op jit(solution)/shard_map/all_to_all | solution.py:28
  120.0 1.1 outputs.1
  121.1 0.6 fusion.12
  121.7 0.6 slice.46
  122.3 0.6 copy.30
  (7 shorter events, 0.1 us)
Async XLA Ops:
  0.6 23.1 %copy-start.10 = (s32[512]{0:T(512)S(1)}, s32[512]{0:T(512)}, u32[]{:S(2)}) copy-start(s32[512]{0:T(512)} %param.13) | copy-start | bytes 6148
  1.4 1.3 %copy-start.1 = (bf16[5,512,256]{2,1,0:T(8,128)(2,1)S(1)}, bf16[5,512,256]{2,1,0:T(8,128)(2,1)}, u32[]{:S(2)}) copy-start(bf16[5,512,256]{2,1,0:T(8,128)(2,1)} %x_ref.3) | copy-start | bytes 3932164
  2.7 1.0 copy-start.3
  3.7 0.7 copy-start.5
  4.4 0.7 copy-start.7
  5.1 17.8 %copy-start.9 = (f32[4,512]{1,0:T(4,128)S(1)}, f32[4,512]{1,0:T(4,128)}, u32[]{:S(2)}) copy-start(f32[4,512]{1,0:T(4,128)} %param.12) | copy-start | bytes 24580
  12.6 20.1 %all-to-all-start = ((bf16[8,5,4,512]{3,2,1,0:T(4,128)(2,1)}), bf16[8,5,4,512]{3,2,1,0:T(4,128)(2,1)S(1)}, u32[]{:S(2)}, u32[]{:S(2)}) async-start(bf16[8,5,4,512]{3,2,1,0:T(4,128)(2,1)} %field.1), calls=%async_computation | async-start | bytes 327680 | tf_op jit(solution)/shard_map/all_to_all | solution.py:28
  33.0 13.9 %copy-start.2 = (bf16[5,512,256]{2,1,0:T(8,128)(2,1)S(1)}, bf16[5,512,256]{2,1,0:T(8,128)(2,1)}, u32[]{:S(2)}) copy-start(bf16[5,512,256]{2,1,0:T(8,128)(2,1)} %x_ref.3) | copy-start | bytes 3932164
  33.1 13.9 %copy-start.4 = (bf16[256,1024]{1,0:T(8,128)(2,1)S(1)}, bf16[256,1024]{1,0:T(8,128)(2,1)}, u32[]{:S(2)}) copy-start(bf16[256,1024]{1,0:T(8,128)(2,1)} %w_ref.5) | copy-start | bytes 1572868
  33.1 13.9 %copy-start.6 = (bf16[4,1024]{1,0:T(4,128)(2,1)S(1)}, bf16[4,1024]{1,0:T(4,128)(2,1)}, u32[]{:S(2)}) copy-start(bf16[4,1024]{1,0:T(4,128)(2,1)} %wo_ref.3) | copy-start | bytes 24580
  33.1 13.9 %copy-start.8 = (f32[1024]{0:T(1024)S(1)}, f32[1024]{0:T(1024)}, u32[]{:S(2)}) copy-start(f32[1024]{0:T(1024)} %param.9) | copy-start | bytes 12292
  34.3 10.6 %all-to-all-start.1 = ((f32[8,8,128]{2,1,0:T(8,128)}), f32[8,8,128]{2,1,0:T(8,128)S(1)}, u32[]{:S(2)}, u32[]{:S(2)}) async-start(f32[8,8,128]{2,1,0:T(8,128)} %broadcast_in_dim.88), calls=%async_computation.1 | async-start | bytes 65536 | tf_op jit(solution)/shard_map/all_to_all | solution.py:28
  99.4 20.5 %all-to-all-start.4 = ((s16[32,72,128]{2,1,0:T(8,128)(2,1)}), s16[32,72,128]{2,1,0:T(8,128)(2,1)S(1)}, u32[]{:S(2)}, u32[]{:S(2)}) async-start(s16[32,72,128]{2,1,0:T(8,128)(2,1)} %mem_sum.1), calls=%async_computation.4 | async-start | bytes 1179648 | tf_op jit(solution)/shard_map/all_to_all | solution.py:28
  104.7 2.5 %copy-start = (bf16[5,512,1024]{2,1,0:T(8,128)(2,1)S(1)}, bf16[5,512,1024]{2,1,0:T(8,128)(2,1)}, u32[]{:S(2)}) copy-start(bf16[5,512,1024]{2,1,0:T(8,128)(2,1)} %get-tuple-element.9.dp_ref) | copy-start | bytes 15728644

commit v3 on v2

v3 whole, which is shorter than its diff:
```python
import functools

import jax
import jax.numpy as jnp
from jax import lax
from jax.experimental import pallas as pl
from jax.experimental.pallas import tpu as pltpu
from jax.sharding import Mesh
from jax.sharding import PartitionSpec as P

epsilon = 1e-06
LAT = ("band", "yl", "x")
GROUP = ("yl", "x")
f32, bf16 = jnp.float32, jnp.bfloat16
NN = (((1,), (0,)), ((), ()))
NT = (((1,), (1,)), ((), ()))
TN = (((0,), (0,)), ((), ()))
LANES = 128
TAIL = 8
EXTRA = 16
IN_VMEM = pl.BlockSpec(memory_space=pltpu.VMEM)
PARAMS = pltpu.CompilerParams(vmem_limit_bytes=40 * 2**20)


def dot(a, b, dims):
    return lax.dot_general(a, b, dims, preferred_element_type=f32)


def exchange(blocks, axes):
    return lax.all_to_all(blocks, axes, 0, 0)


def quantize(block):
    top = jnp.max(jnp.abs(block), keepdims=True)
    exponent = jnp.clip(jnp.ceil(jnp.log2(jnp.maximum(top, 1e-33))), -110.0, 110.0)
    whole = jnp.clip(jnp.round(block * jnp.exp2(15.0 - exponent)), -32767.0, 32767.0)
    return whole.astype(jnp.int32), exponent.astype(jnp.int32)


def encode(block, tail):
    row = lax.broadcasted_iota(jnp.int32, tail.shape, 0)
    codes, exponent = quantize(block)
    tail_codes, tail_exponent = quantize(jnp.where(row < TAIL - 2, tail, 0.0))
    last = jnp.where(
        row == TAIL - 2, exponent, jnp.where(row == TAIL - 1, tail_exponent, tail_codes)
    )
    return jnp.concatenate([codes, last], axis=0).astype(jnp.int16)


def decode(chunk):
    values = chunk.astype(jnp.int32).astype(f32)
    rows = values.shape[0] - TAIL
    block = values[:rows] * jnp.exp2(values[rows + TAIL - 2 : rows + TAIL - 1] - 15.0)
    tail = values[rows:] * jnp.exp2(values[rows + TAIL - 1 :] - 15.0)
    row = lax.broadcasted_iota(jnp.int32, tail.shape, 0)
    return block, jnp.where(row < TAIL - 2, tail, 0.0)


def blocks(members, hid):
    step = hid // 4
    return [(m, slice(k * step, (k + 1) * step)) for m in range(members) for k in range(4)]


def field_kernel(
    x_hbm, w_hbm, b_hbm, wo_hbm, bo_hbm, f_ref, x_ref, w_ref, b_ref, wo_ref, bo_ref, sems
):
    members = x_ref.shape[0]
    sources = [(w_hbm, w_ref), (x_hbm.at[0], x_ref.at[0]), (b_hbm, b_ref), (wo_hbm, wo_ref)]
    sources.append((bo_hbm, bo_ref))
    sources += [(x_hbm.at[m], x_ref.at[m]) for m in range(1, members)]
    loads = [
        pltpu.make_async_copy(source, target, sems.at[i])
        for i, (source, target) in enumerate(sources)
    ]
    for load in loads:
        load.start()
    for load in loads[:5]:
        load.wait()
    nvars, hid = wo_ref.shape
    square = (nvars, nvars)
    diagonal = lax.broadcasted_iota(jnp.int32, square, 0) == lax.broadcasted_iota(
        jnp.int32, square, 1
    )
    bias = jnp.sum(jnp.where(diagonal, bo_ref[...], 0.0), axis=1, keepdims=True)
    totals = [bias] * members
    waiting = None

    def second_layer(m, cols, hidden):
        totals[m] = totals[m] + dot(wo_ref[:, cols], hidden, NT)

    for m, cols in blocks(members, hid):
        if m > 0 and cols.start == 0:
            loads[4 + m].wait()
        half = 0.5 * (dot(x_ref[m], w_ref[:, cols], NN) + b_ref[:, cols])
        hidden = (half * jnp.tanh(half) + half).astype(bf16)
        if waiting is not None:
            second_layer(*waiting)
        waiting = (m, cols, hidden)
    second_layer(*waiting)
    for m in range(members):
        field = totals[m].astype(bf16)
        for copy in range(f_ref.shape[0]):
            f_ref[copy, m] = field


def forward(latent, w, b, wo, bo, copies):
    pinned = [pltpu.with_memory_space_constraint(a, pltpu.HBM) for a in (latent, w, b.reshape(1, -1), wo, bo.reshape(1, -1))]
    members, cells, _ = latent.shape
    nvars, hid = wo.shape
    in_hbm = pl.BlockSpec(memory_space=pltpu.HBM)
    return pl.pallas_call(
        field_kernel,
        in_specs=[in_hbm] * 5,
        out_shape=[
            jax.ShapeDtypeStruct((copies, members, nvars, cells), bf16),
            pltpu.VMEM(latent.shape, bf16),
            pltpu.VMEM(w.shape, bf16),
            pltpu.VMEM((1, hid), f32),
            pltpu.VMEM(wo.shape, bf16),
        ],
        out_specs=[IN_VMEM] * 5,
        scratch_shapes=[pltpu.VMEM((1, nvars), f32), pltpu.SemaphoreType.DMA((4 + members,))],
        compiler_params=PARAMS,
        name="field",
    )(*pinned)


def member_block(*dims):
    return pl.BlockSpec((1, *dims), lambda i: (i, 0, 0))


def whole(array):
    return pl.BlockSpec(array.shape, lambda i: (0,) * array.ndim)


def backward_kernel(
    x_ref, w_ref, b_ref, wo_ref, g_ref, dp_hbm, pay_ref, dp_ref, acc, small, xt, sems
):
    members, cells, width = x_ref.shape
    nvars, hid = wo_ref.shape
    bias = None
    for m in range(members):
        sums = jnp.sum(g_ref[m].astype(f32), axis=1, keepdims=True)
        bias = sums if bias is None else bias + sums
        xt[m, :width] = x_ref[m].T
        xt[m, width:] = jnp.ones((EXTRA, cells), bf16)

    saves = [
        pltpu.make_async_copy(dp_ref.at[m], dp_hbm.at[m], sems.at[m]) for m in range(members)
    ]

    def add(m, cols, dp, hidden):
        d_in, d_out = dot(xt[m], dp, NN), dot(g_ref[m], hidden, NN)
        if m == 0:
            acc[:, cols], small[:, cols] = d_in, d_out
        else:
            acc[:, cols] += d_in
            small[:, cols] += d_out

    waiting = None
    for m, cols in blocks(members, hid):
        pre = dot(x_ref[m], w_ref[:, cols], NN) + b_ref[:, cols]
        sig = 0.5 * jnp.tanh(0.5 * pre) + 0.5
        act = pre * sig
        slope = act * (1.0 - sig) + sig
        dp = (dot(g_ref[m], wo_ref[:, cols], TN) * slope).astype(bf16)
        dp_ref[m, :, cols] = dp
        if cols.stop == hid:
            saves[m].start()
        if waiting is not None:
            add(*waiting)
        waiting = (m, cols, dp, act.astype(bf16))
    add(*waiting)

    n_col = hid // LANES
    rows = width // (pay_ref.shape[0] // n_col)
    row = lax.broadcasted_iota(jnp.int32, (TAIL, LANES), 0)
    empty = jnp.zeros((TAIL - nvars, LANES), f32)
    for cb in range(n_col):
        lanes = slice(cb * LANES, (cb + 1) * LANES)
        tails = [jnp.concatenate([small[:, lanes], empty], axis=0)]
        tails.append(jnp.where(row == nvars, acc[width : width + 1, lanes], 0.0))
        sums = bias[cb : cb + 1] if cb < nvars else jnp.zeros((1, 1), f32)
        tails.append(jnp.where(row == nvars + 1, sums, 0.0))
        tails.append(jnp.zeros((TAIL, LANES), f32))
        for rb, tail in enumerate(tails):
            pay_ref[rb * n_col + cb] = encode(acc[rb * rows : (rb + 1) * rows, lanes], tail)
    for save in saves:
        save.wait()


def backward(latent, w, b, wo, g, chunks):
    members, cells, width = latent.shape
    nvars, hid = wo.shape
    return pl.pallas_call(
        backward_kernel,
        in_specs=[IN_VMEM] * 5,
        out_shape=[
            pltpu.HBM((members, cells, hid), bf16),
            pltpu.VMEM((chunks, width * hid // (chunks * LANES) + TAIL, LANES), jnp.int16),
        ],
        out_specs=[pl.BlockSpec(memory_space=pltpu.HBM), IN_VMEM],
        scratch_shapes=[
            pltpu.VMEM((members, cells, hid), bf16),
            pltpu.VMEM((width + EXTRA, hid), f32),
            pltpu.VMEM((nvars, hid), f32),
            pltpu.VMEM((members, width + EXTRA, cells), bf16),
            pltpu.SemaphoreType.DMA((members,)),
        ],
        compiler_params=PARAMS,
        name="backward",
    )(latent, w, b, wo, g)


def down_kernel(dp_ref, w_ref, o_ref):
    o_ref[0] = dot(dp_ref[0], w_ref[...], NT).astype(bf16)


def down(dp, w):
    members, cells, hid = dp.shape
    width = w.shape[0]
    return pl.pallas_call(
        down_kernel,
        grid=(members,),
        in_specs=[member_block(cells, hid), whole(w)],
        out_specs=member_block(cells, width),
        out_shape=jax.ShapeDtypeStruct((members, cells, width), bf16),
        compiler_params=PARAMS,
        name="d_latent",
    )(pltpu.with_memory_space_constraint(dp, pltpu.HBM), w)


def reduce_kernel(scale, in_ref, out_ref):
    total, tail = decode(in_ref[0])
    for source in range(1, in_ref.shape[0]):
        block, more = decode(in_ref[source])
        total, tail = total + block, tail + more
    chunk = encode(total * scale, tail * scale)
    for copy in range(out_ref.shape[0]):
        out_ref[copy] = chunk


def reduce_and_copy(received, copies, scale, name):
    return pl.pallas_call(
        functools.partial(reduce_kernel, scale),
        out_shape=jax.ShapeDtypeStruct((copies, *received.shape[1:]), jnp.int16),
        compiler_params=PARAMS,
        name=name,
    )(received)


def spread_kernel(in_ref, d_in_ref, d_out_ref, d_bin_ref, d_bout_ref):
    n_col = d_in_ref.shape[1] // LANES
    nvars = d_out_ref.shape[0]
    rows = in_ref.shape[1] - TAIL
    for cb in range(n_col):
        lanes = slice(cb * LANES, (cb + 1) * LANES)
        tails = None
        for rb in range(in_ref.shape[0] // n_col):
            block, tail = decode(in_ref[rb * n_col + cb])
            d_in_ref[rb * rows : (rb + 1) * rows, lanes] = block
            tails = tail if tails is None else tails + tail
        d_out_ref[:, lanes] = tails[:nvars]
        d_bin_ref[pl.ds(cb * LANES, LANES)] = tails[nvars]
        if cb < nvars:
            d_bout_ref[cb] = tails[nvars + 1, 0]


def spread_out(received, width, hid, nvars):
    return pl.pallas_call(
        spread_kernel,
        out_shape=[
            jax.ShapeDtypeStruct((width, hid), f32),
            jax.ShapeDtypeStruct((nvars, hid), f32),
            jax.ShapeDtypeStruct((hid,), f32),
            jax.ShapeDtypeStruct((nvars,), f32),
        ],
        out_specs=[IN_VMEM] * 3 + [pl.BlockSpec(memory_space=pltpu.SMEM)],
        compiler_params=PARAMS,
        name="outputs",
    )(received)


def local(latent, in_weight, in_bias, out_weight, out_bias, observed, patch_of_cell):
    members_here, cells_here, width = latent.shape
    nvars, hid = out_weight.shape
    n_mem = lax.axis_size("mem")
    n_lat = lax.axis_size(LAT)
    n_group = lax.axis_size(GROUP)
    members = members_here * n_mem
    entries = float(nvars * 4 * cells_here)
    highest = lax.Precision.HIGHEST
    copies, latent, in_weight, in_bias, out_weight = forward(
        latent, in_weight, in_bias, out_weight, out_bias, n_mem
    )
    all_fields = exchange(copies, "mem").reshape(members, nvars, cells_here).astype(f32)
    own_field = copies[0].astype(f32)
    own_patch = patch_of_cell - 2 * lax.axis_index("band")
    in_patch = (own_patch[:, None] == jnp.arange(2, dtype=jnp.int32)[None, :]).astype(f32)
    misfit = own_field - observed[None]
    obs_part = jnp.dot(jnp.sum(misfit * misfit, axis=1), in_patch, precision=highest)
    diff = own_field[:, None] - all_fields[None]
    squared = jnp.sum(diff * diff, axis=2)
    pair_part = jnp.einsum("mnc,cp->mnp", squared, in_patch, precision=highest)
    flat = jnp.concatenate([pair_part.reshape(-1), obs_part.reshape(-1)])
    room = -(-flat.size // 1024) * 1024
    flat = jnp.pad(flat, (0, room - flat.size)).reshape(-1, 128)
    sums = exchange(jnp.broadcast_to(flat[None], (n_group, *flat.shape)), GROUP)
    sums = jnp.sum(sums, axis=0).reshape(-1)
    pair_sum = sums[: members_here * members * 2].reshape(members_here, members, 2)
    obs_sum = sums[members_here * members * 2 :][: members_here * 2].reshape(members_here, 2)
    spread = jnp.sqrt(obs_sum / entries + epsilon)
    dist = jnp.sqrt(pair_sum / entries + epsilon)
    own_ids = lax.axis_index("mem") * members_here + jnp.arange(members_here, dtype=jnp.int32)
    other_ids = jnp.arange(members, dtype=jnp.int32)
    inv_dist = jnp.where(
        (own_ids[:, None] != other_ids[None, :])[:, :, None], 1.0 / dist, jnp.float32(0.0)
    )
    first = (own_patch == 0)[None, None, :]
    cell_w = jnp.where(first, inv_dist[:, :, :1], inv_dist[:, :, 1:])
    cell_spread = jnp.where(first[0], spread[:, :1], spread[:, 1:])
    pulled = jnp.sum(cell_w[:, :, None, :] * diff, axis=1)
    grad_field = (misfit / cell_spread[:, None, :] - pulled / members).astype(bf16)
    d_preact, payload = backward(latent, in_weight, in_bias, out_weight, grad_field, n_lat)
    d_latent = down(d_preact, in_weight)
    scale = 1.0 / (members * cells_here * n_lat) ** 0.5
    payload = reduce_and_copy(exchange(payload, LAT), n_mem, 1.0, "lat_sum")
    payload = reduce_and_copy(exchange(payload, "mem"), n_lat, scale, "mem_sum")
    return (d_latent, *spread_out(exchange(payload, LAT), width, hid, nvars))


def solution(mesh):
    n_mem, n_lat, n_rep = (mesh.shape[a] for a in ("mem", "lat", "rep"))
    split = Mesh(
        mesh.devices.reshape(n_mem, n_lat // 8, 2, 4, n_rep), ("mem", "band", "yl", "x", "rep")
    )
    placed = (P(("rep", "mem"), LAT, None), P(), P(), P(), P(), P("rep", LAT), P(LAT))
    return jax.shard_map(
        local,
        mesh=split,
        in_specs=placed,
        out_specs=(
            P(("rep", "mem"), LAT, None),
            P("rep", None),
            P("rep", None),
            P("rep"),
            P("rep"),
        ),
        check_vma=False,
    )
```

time: 124 us -> 107 us (0.86)
  local copies, waits for them, and re-layouts: 10.4 us -> 1.65 us
  Pallas kernels: 29 us -> 20.9 us
    pallas_call x3, Pallas kernels: 26.5 us -> 18.3 us  [the longest x1 6.53 us: backward(): pl.pallas_call(backward_kernel, in_specs=[IN_VMEM] * 5, out_shape=[pltpu....]
    unnamed x23 -> x4, local copies, waits for them, and re-layouts: 6.85 us -> 0.01 us
  transfers between devices with their start and end apart: 3 -> 3, of which waited for: 3 -> 3; matrix products, arithmetic and copies ran while one was open for 1% -> 2% of each run, Pallas kernels for 3% -> 6%
where the time goes in v3:
time: 107 us; the launch traced here: 106 us
  blocking collectives  35.6 us (33%)
  waiting for transfers between devices  22 us (21%)
  starting transfers between devices  21.3 us (20%)
  Pallas kernels  20.9 us (20%)
  other arithmetic  3.21 us (3%)
  local copies, waits for them, and re-layouts  1.65 us (2%)
    all_to_all x2, blocking collectives, exchange(): return lax.all_to_all(blocks, axes, 0, 0)  35.6 us
    all_to_all x3, waiting for transfers between devices, exchange(): return lax.all_to_all(blocks, axes, 0, 0)  22 us
    all_to_all x3, starting transfers between devices, exchange(): return lax.all_to_all(blocks, axes, 0, 0)  21.3 us
    pallas_call x1, Pallas kernels, backward(): pl.pallas_call(backward_kernel, in_specs=[IN_VMEM] * 5, out_shape=[pltpu....  6.53 us
    pallas_call x1, Pallas kernels, down(): pl.pallas_call(down_kernel, grid=(members,), in_specs=[member_block(cells...  6.06 us
    pallas_call x1, Pallas kernels, forward(): pl.pallas_call(field_kernel, in_specs=[in_hbm] * 5, out_shape=[jax.ShapeD...  5.7 us
  transfers between devices with their start and end apart: 3, of which 3 were waited for; matrix products, arithmetic and copies ran while one was open for 2% of the time, Pallas kernels for 6%

profile of v3, /device:TPU:8, one launch (start us, length us, event | category | flops | bytes accessed | tf_op | source)
XLA Modules:
  0.0 105.9 jit_solution(1185649235736696453)
XLA Ops:
  0.6 0.0 copy-start
  0.6 0.0 copy-start.1
  0.7 5.7 %field.1 = (bf16[8,5,4,512]{3,2,1,0:T(4,128)(2,1)}, bf16[5,512,256]{2,1,0:T(8,128)(2,1)S(1)}, bf16[256,1024]{1,0:T(8,128)(2,1)S(1)}, f32[1,1024]{1,0:T(1,128)S(1)}, bf16[4,1024]{1,0:T(4,128)(2,1)S(1)}) custom-call(bf16[5,512,256]{2,1,0:T(8,128)(2,1)} %x_hbm.1, bf16[256,1024]{1,0:T(8,128)(2,1)} %w_hbm.1, f32[1,1024]{1,0:T(1,128)} %bitcast.19, ...), custom_call_target="tpu_custom_call" | custom-call | tf_op jit(solution)/shard_map/field/pallas_call | solution.py:111
  6.4 10.3 %all-to-all-start = ((bf16[8,5,4,512]{3,2,1,0:T(4,128)(2,1)}), bf16[8,5,4,512]{3,2,1,0:T(4,128)(2,1)S(1)}, u32[]{:S(2)}, u32[]{:S(2)}) async-start(bf16[8,5,4,512]{3,2,1,0:T(4,128)(2,1)} %get-tuple-element.20), calls=%async_computation | async-start | bytes 327680 | tf_op jit(solution)/shard_map/all_to_all | solution.py:30
  16.7 0.0 copy-done
  16.7 0.8 multiply_reduce_fusion
  17.5 0.0 copy-done.1
  17.5 0.1 fusion.8
  17.6 0.1 reshape.117
  17.7 0.7 bitcast_convert_fusion.1
  18.4 8.0 %all-to-all-done = bf16[8,5,4,512]{3,2,1,0:T(4,128)(2,1)S(1)} async-done(((bf16[8,5,4,512]{3,2,1,0:T(4,128)(2,1)}), bf16[8,5,4,512]{3,2,1,0:T(4,128)(2,1)S(1)}, u32[]{:S(2)}, u32[]{:S(2)}) %all-to-all-start) | async-done | bytes 163872 | tf_op jit(solution)/shard_map/all_to_all | solution.py:30
  26.5 0.1 copy.17
  26.6 0.2 fusion
  26.8 0.3 fusion.3
  27.1 0.1 reshape.116
  27.3 0.1 fusion.7
  27.3 0.6 broadcast_in_dim.88
  28.0 5.8 %all-to-all-start.1 = ((f32[8,8,128]{2,1,0:T(8,128)}), f32[8,8,128]{2,1,0:T(8,128)S(1)}, u32[]{:S(2)}, u32[]{:S(2)}) async-start(f32[8,8,128]{2,1,0:T(8,128)} %broadcast_in_dim.88), calls=%async_computation.1 | async-start | bytes 65536 | tf_op jit(solution)/shard_map/all_to_all | solution.py:30
  33.7 0.1 iota_compare_fusion.1
  33.8 4.8 %all-to-all-done.1 = f32[8,8,128]{2,1,0:T(8,128)S(1)} async-done(((f32[8,8,128]{2,1,0:T(8,128)}), f32[8,8,128]{2,1,0:T(8,128)S(1)}, u32[]{:S(2)}, u32[]{:S(2)}) %all-to-all-start.1) | async-done | bytes 32800 | tf_op jit(solution)/shard_map/all_to_all | solution.py:30
  38.6 0.2 slice.27
  38.8 0.1 sqrt.10
  38.9 0.1 broadcast_select_fusion.1
  39.0 0.2 slice_reduce_fusion.1
  39.2 0.2 slice_reduce_fusion.3
  39.4 0.1 broadcast_select_fusion
  39.6 0.3 fusion.1
  39.8 0.1 broadcast_select_fusion.2
  39.9 0.8 fusion.2.g_ref
  40.6 6.5 %backward.1 = (bf16[5,512,1024]{2,1,0:T(8,128)(2,1)}, s16[32,72,128]{2,1,0:T(8,128)(2,1)S(1)}) custom-call(bf16[5,512,256]{2,1,0:T(8,128)(2,1)S(1)} %get-tuple-element.16.x_ref, bf16[256,1024]{1,0:T(8,128)(2,1)S(1)} %get-tuple-element.17.w_ref, f32[1,1024]{1,0:T(1,128)S(1)} %get-tuple-element.18.b_ref, bf16[4,1024]{1,0:T(4,128)(2,1)S(1)} %get-tuple-element.19.wo_ref, ...), custom_call_target="tpu_custom_call" | custom-call | tf_op jit(solution)/shard_map/backward/pallas_call | solution.py:195
  47.2 23.4 %all_to_all.25.in_ref = s16[32,72,128]{2,1,0:T(8,128)(2,1)S(1)} all-to-all(s16[32,72,128]{2,1,0:T(8,128)(2,1)S(1)} %get-tuple-element.22), channel_id=1, replica_groups=mesh['mem'=8,'band'=4,'yl'=2,'x'=4,'rep'=2] {'band','yl','x'}, dimensions={0} | all-to-all | bytes 1179648 | tf_op jit(solution)/shard_map/all_to_all | solution.py:30
  70.6 0.3 lat_sum.1
  70.9 12.2 %all_to_all.26.in_ref = s16[8,72,128]{2,1,0:T(8,128)(2,1)S(1)} all-to-all(s16[8,72,128]{2,1,0:T(8,128)(2,1)S(1)} %lat_sum.1), channel_id=1, replica_groups=mesh['mem'=8,'band'=4,'yl'=2,'x'=4,'rep'=2] {'mem'}, dimensions={0} | all-to-all | bytes 294912 | tf_op jit(solution)/shard_map/all_to_all | solution.py:30
  83.1 1.1 %mem_sum.1 = s16[32,72,128]{2,1,0:T(8,128)(2,1)} custom-call(s16[8,72,128]{2,1,0:T(8,128)(2,1)S(1)} %all_to_all.26.in_ref), custom_call_target="tpu_custom_call" | custom-call | tf_op jit(solution)/shard_map/mem_sum/pallas_call | solution.py:244
  84.2 5.2 %all-to-all-start.4 = ((s16[32,72,128]{2,1,0:T(8,128)(2,1)}), s16[32,72,128]{2,1,0:T(8,128)(2,1)S(1)}, u32[]{:S(2)}, u32[]{:S(2)}) async-start(s16[32,72,128]{2,1,0:T(8,128)(2,1)} %mem_sum.1), calls=%async_computation.4 | async-start | bytes 1179648 | tf_op jit(solution)/shard_map/all_to_all | solution.py:30
  89.4 6.1 %d_latent.1 = bf16[5,512,256]{2,1,0:T(8,128)(2,1)} custom-call(bf16[5,512,1024]{2,1,0:T(8,128)(2,1)} %get-tuple-element.21.dp_ref, bf16[256,1024]{1,0:T(8,128)(2,1)S(1)} %get-tuple-element.17.w_ref), custom_call_target="tpu_custom_call" | custom-call | tf_op jit(solution)/shard_map/d_latent/pallas_call | solution.py:222
  95.5 9.2 %all-to-all-done.4.in_ref = s16[32,72,128]{2,1,0:T(8,128)(2,1)S(1)} async-done(((s16[32,72,128]{2,1,0:T(8,128)(2,1)}), s16[32,72,128]{2,1,0:T(8,128)(2,1)S(1)}, u32[]{:S(2)}, u32[]{:S(2)}) %all-to-all-start.4) | async-done | bytes 589856 | tf_op jit(solution)/shard_map/all_to_all | solution.py:30
  104.7 1.2 %outputs.1 = (f32[256,1024]{1,0:T(8,128)}, f32[4,1024]{1,0:T(4,128)}, f32[1024]{0:T(1024)}, f32[4]{0:T(128)}) custom-call(s16[32,72,128]{2,1,0:T(8,128)(2,1)S(1)} %all-to-all-done.4.in_ref), custom_call_target="tpu_custom_call" | custom-call | tf_op jit(solution)/shard_map/outputs/pallas_call | solution.py:270
  (6 shorter events, 0.1 us)
Async XLA Ops:
  0.6 16.1 %copy-start = (f32[4,512]{1,0:T(4,128)S(1)}, f32[4,512]{1,0:T(4,128)}, u32[]{:S(2)}) copy-start(f32[4,512]{1,0:T(4,128)} %param.12) | copy-start | bytes 24580
  0.6 16.8 %copy-start.1 = (s32[512]{0:T(512)S(1)}, s32[512]{0:T(512)}, u32[]{:S(2)}) copy-start(s32[512]{0:T(512)} %param.13) | copy-start | bytes 6148
  6.4 20.1 %all-to-all-start = ((bf16[8,5,4,512]{3,2,1,0:T(4,128)(2,1)}), bf16[8,5,4,512]{3,2,1,0:T(4,128)(2,1)S(1)}, u32[]{:S(2)}, u32[]{:S(2)}) async-start(bf16[8,5,4,512]{3,2,1,0:T(4,128)(2,1)} %get-tuple-element.20), calls=%async_computation | async-start | bytes 327680 | tf_op jit(solution)/shard_map/all_to_all | solution.py:30
  28.0 10.6 %all-to-all-start.1 = ((f32[8,8,128]{2,1,0:T(8,128)}), f32[8,8,128]{2,1,0:T(8,128)S(1)}, u32[]{:S(2)}, u32[]{:S(2)}) async-start(f32[8,8,128]{2,1,0:T(8,128)} %broadcast_in_dim.88), calls=%async_computation.1 | async-start | bytes 65536 | tf_op jit(solution)/shard_map/all_to_all | solution.py:30
  84.2 20.5 %all-to-all-start.4 = ((s16[32,72,128]{2,1,0:T(8,128)(2,1)}), s16[32,72,128]{2,1,0:T(8,128)(2,1)S(1)}, u32[]{:S(2)}, u32[]{:S(2)}) async-start(s16[32,72,128]{2,1,0:T(8,128)(2,1)} %mem_sum.1), calls=%async_computation.4 | async-start | bytes 1179648 | tf_op jit(solution)/shard_map/all_to_all | solution.py:30

commit v4 on v3

--- a/solution.py
+++ b/solution.py
@@ -133,24 +133,52 @@
     return pl.BlockSpec(array.shape, lambda i: (0,) * array.ndim)
 
 
+def gradients(entries, n_members, sums_ref, keep_ref, own_ref, misfit_ref, rhs_ref):
+    nvars = own_ref.shape[0]
+    total = sums_ref[0]
+    for source in range(1, sums_ref.shape[0]):
+        total = total + sums_ref[source]
+    weights = keep_ref[...] / jnp.sqrt(total / entries + epsilon)
+    high = weights.astype(bf16).astype(f32)
+    middle = (weights - high).astype(bf16).astype(f32)
+    pieces = [high, middle, weights - high - middle, jnp.zeros_like(high)]
+    pieces = jnp.concatenate(pieces, axis=0).astype(bf16)
+    rows = weights.shape[0]
+
+    def per_cell(i):
+        out = dot(pieces, rhs_ref[i], NN)
+        return out[:rows] + out[rows : 2 * rows] + out[2 * rows : 3 * rows]
+
+    row_total, over_spread = per_cell(nvars), per_cell(nvars + 1)
+    parts = []
+    for v in range(nvars):
+        pulled = own_ref[v] * row_total - per_cell(v)
+        parts.append(misfit_ref[v] * over_spread - pulled / n_members)
+    return [
+        jnp.concatenate([part[m : m + 1] for part in parts], axis=0).astype(bf16)
+        for m in range(rows)
+    ]
+
+
 def backward_kernel(
-    x_ref, w_ref, b_ref, wo_ref, g_ref, dp_hbm, pay_ref, dp_ref, acc, small, xt, sems
+    entries, n_members, x_ref, w_ref, b_ref, wo_ref, sums_ref, keep_ref, own_ref, misfit_ref, rhs_ref,
+    dp_hbm, pay_ref, dp_ref, acc, small, xt, sems,
 ):
     members, cells, width = x_ref.shape
     nvars, hid = wo_ref.shape
+    grads = gradients(entries, n_members, sums_ref, keep_ref, own_ref, misfit_ref, rhs_ref)
     bias = None
     for m in range(members):
-        sums = jnp.sum(g_ref[m].astype(f32), axis=1, keepdims=True)
+        sums = jnp.sum(grads[m].astype(f32), axis=1, keepdims=True)
         bias = sums if bias is None else bias + sums
         xt[m, :width] = x_ref[m].T
         xt[m, width:] = jnp.ones((EXTRA, cells), bf16)
-
     saves = [
         pltpu.make_async_copy(dp_ref.at[m], dp_hbm.at[m], sems.at[m]) for m in range(members)
     ]
 
     def add(m, cols, dp, hidden):
-        d_in, d_out = dot(xt[m], dp, NN), dot(g_ref[m], hidden, NN)
+        d_in, d_out = dot(xt[m], dp, NN), dot(grads[m], hidden, NN)
         if m == 0:
             acc[:, cols], small[:, cols] = d_in, d_out
         else:
@@ -163,7 +191,7 @@
         sig = 0.5 * jnp.tanh(0.5 * pre) + 0.5
         act = pre * sig
         slope = act * (1.0 - sig) + sig
-        dp = (dot(g_ref[m], wo_ref[:, cols], TN) * slope).astype(bf16)
+        dp = (dot(grads[m], wo_ref[:, cols], TN) * slope).astype(bf16)
         dp_ref[m, :, cols] = dp
         if cols.stop == hid:
             saves[m].start()
@@ -189,12 +217,12 @@
         save.wait()
 
 
-def backward(latent, w, b, wo, g, chunks):
+def backward(latent, w, b, wo, field_operands, entries, n_members, chunks):
     members, cells, width = latent.shape
     nvars, hid = wo.shape
     return pl.pallas_call(
-        backward_kernel,
-        in_specs=[IN_VMEM] * 5,
+        functools.partial(backward_kernel, entries, n_members),
+        in_specs=[IN_VMEM] * (4 + len(field_operands)),
         out_shape=[
             pltpu.HBM((members, cells, hid), bf16),
             pltpu.VMEM((chunks, width * hid // (chunks * LANES) + TAIL, LANES), jnp.int16),
@@ -209,7 +237,7 @@
         ],
         compiler_params=PARAMS,
         name="backward",
-    )(latent, w, b, wo, g)
+    )(latent, w, b, wo, *field_operands)
 
 
 def down_kernel(dp_ref, w_ref, o_ref):
@@ -301,27 +329,39 @@
     obs_part = jnp.dot(jnp.sum(misfit * misfit, axis=1), in_patch, precision=highest)
     diff = own_field[:, None] - all_fields[None]
     squared = jnp.sum(diff * diff, axis=2)
-    pair_part = jnp.einsum("mnc,cp->mnp", squared, in_patch, precision=highest)
-    flat = jnp.concatenate([pair_part.reshape(-1), obs_part.reshape(-1)])
-    room = -(-flat.size // 1024) * 1024
-    flat = jnp.pad(flat, (0, room - flat.size)).reshape(-1, 128)
+    pair_part = jnp.einsum("mnc,cp->mpn", squared, in_patch, precision=highest)
+    flat = jnp.concatenate([pair_part.reshape(members_here, 2 * members), obs_part], axis=1)
+    used = 2 * members + 2
+    flat = jnp.pad(flat, ((0, TAIL - members_here), (0, LANES - used)))
     sums = exchange(jnp.broadcast_to(flat[None], (n_group, *flat.shape)), GROUP)
-    sums = jnp.sum(sums, axis=0).reshape(-1)
-    pair_sum = sums[: members_here * members * 2].reshape(members_here, members, 2)
-    obs_sum = sums[members_here * members * 2 :][: members_here * 2].reshape(members_here, 2)
-    spread = jnp.sqrt(obs_sum / entries + epsilon)
-    dist = jnp.sqrt(pair_sum / entries + epsilon)
-    own_ids = lax.axis_index("mem") * members_here + jnp.arange(members_here, dtype=jnp.int32)
-    other_ids = jnp.arange(members, dtype=jnp.int32)
-    inv_dist = jnp.where(
-        (own_ids[:, None] != other_ids[None, :])[:, :, None], 1.0 / dist, jnp.float32(0.0)
-    )
-    first = (own_patch == 0)[None, None, :]
-    cell_w = jnp.where(first, inv_dist[:, :, :1], inv_dist[:, :, 1:])
-    cell_spread = jnp.where(first[0], spread[:, :1], spread[:, 1:])
-    pulled = jnp.sum(cell_w[:, :, None, :] * diff, axis=1)
-    grad_field = (misfit / cell_spread[:, None, :] - pulled / members).astype(bf16)
-    d_preact, payload = backward(latent, in_weight, in_bias, out_weight, grad_field, n_lat)
+    masks = in_patch.T
+    by_var = all_fields.transpose(1, 0, 2)
+    pairs = (by_var[:, None] * masks[None, :, None]).reshape(nvars, 2 * members, cells_here)
+    ones = jnp.broadcast_to(masks[:, None], (2, members, cells_here))
+    ones = ones.reshape(1, 2 * members, cells_here)
+    upper = jnp.concatenate([pairs, ones, jnp.zeros_like(ones)], axis=0)
+    lower = jnp.zeros((nvars + 2, 2, cells_here), f32).at[nvars + 1].set(masks)
+    rhs = jnp.concatenate([upper, lower], axis=1)
+    rhs = jnp.pad(rhs, ((0, 0), (0, LANES - used), (0, 0))).astype(bf16)
+    row = lax.broadcasted_iota(jnp.int32, (TAIL, LANES), 0)
+    lane = lax.broadcasted_iota(jnp.int32, (TAIL, LANES), 1)
+    own_id = lax.axis_index("mem") * members_here + row
+    another = (lane < 2 * members) & (lane % members != own_id)
+    wanted = another | ((lane >= 2 * members) & (lane < used))
+    keep = (wanted & (row < members_here)).astype(f32)
+    fill = ((0, 0), (0, TAIL - members_here), (0, 0))
+    own = jnp.pad(own_field.transpose(1, 0, 2), fill)
+    off = jnp.pad(misfit.transpose(1, 0, 2), fill)
+    d_preact, payload = backward(
+        latent,
+        in_weight,
+        in_bias,
+        out_weight,
+        (sums, keep, own, off, rhs),
+        entries,
+        members,
+        n_lat,
+    )
     d_latent = down(d_preact, in_weight)
     scale = 1.0 / (members * cells_here * n_lat) ** 0.5
     payload = reduce_and_copy(exchange(payload, LAT), n_mem, 1.0, "lat_sum")

time: 107 us -> 105 us (0.981)
  other arithmetic: 3.21 us -> 0.69 us
    convert_element_type x2, other arithmetic: 1.5 us -> 0.08 us  [the longest x1 0.08 us: local(): keep = (wanted & (row < members_here)).astype(f32)]
where the time goes in v4:
time: 105 us; the launch traced here: 104 us
  blocking collectives  35.6 us (34%)
  waiting for transfers between devices  22 us (21%)
  starting transfers between devices  21.3 us (20%)
  Pallas kernels  21 us (20%)
  local copies, waits for them, and re-layouts  2.05 us (2%)
    all_to_all x2, blocking collectives, exchange(): return lax.all_to_all(blocks, axes, 0, 0)  35.6 us
    all_to_all x3, waiting for transfers between devices, exchange(): return lax.all_to_all(blocks, axes, 0, 0)  22 us
    all_to_all x3, starting transfers between devices, exchange(): return lax.all_to_all(blocks, axes, 0, 0)  21.3 us
    pallas_call x1, Pallas kernels, backward(): pl.pallas_call(functools.partial(backward_kernel, entries, n_members), in...  6.68 us
    pallas_call x1, Pallas kernels, down(): pl.pallas_call(down_kernel, grid=(members,), in_specs=[member_block(cells...  6.07 us
    pallas_call x1, Pallas kernels, forward(): pl.pallas_call(field_kernel, in_specs=[in_hbm] * 5, out_shape=[jax.ShapeD...  5.69 us
  transfers between devices with their start and end apart: 3, of which 3 were waited for; matrix products, arithmetic and copies ran while one was open for 2% of the time, Pallas kernels for 6%

profile of v4, /device:TPU:8, one launch (start us, length us, event | category | flops | bytes accessed | tf_op | source)
XLA Modules:
  0.0 104.1 jit_solution(12805855547835189140)
XLA Ops:
  0.6 0.0 copy-start.1
  0.6 0.0 copy-start
  0.7 5.7 %field.1 = (bf16[8,5,4,512]{3,2,1,0:T(4,128)(2,1)}, bf16[5,512,256]{2,1,0:T(8,128)(2,1)S(1)}, bf16[256,1024]{1,0:T(8,128)(2,1)S(1)}, f32[1,1024]{1,0:T(1,128)S(1)}, bf16[4,1024]{1,0:T(4,128)(2,1)S(1)}) custom-call(bf16[5,512,256]{2,1,0:T(8,128)(2,1)} %x_hbm.1, bf16[256,1024]{1,0:T(8,128)(2,1)} %w_hbm.1, f32[1,1024]{1,0:T(1,128)} %bitcast.37, ...), custom_call_target="tpu_custom_call" | custom-call | tf_op jit(solution)/shard_map/field/pallas_call | solution.py:111
  6.4 10.3 %all-to-all-start = ((bf16[8,5,4,512]{3,2,1,0:T(4,128)(2,1)}), bf16[8,5,4,512]{3,2,1,0:T(4,128)(2,1)S(1)}, u32[]{:S(2)}, u32[]{:S(2)}) async-start(bf16[8,5,4,512]{3,2,1,0:T(4,128)(2,1)} %get-tuple-element.32), calls=%async_computation | async-start | bytes 327680 | tf_op jit(solution)/shard_map/all_to_all | solution.py:30
  16.7 0.0 copy-done.1
  16.8 1.0 copy.16
  17.8 0.0 copy-done
  17.9 0.1 fusion.8.keep_ref
  18.0 0.1 fusion.4
  18.1 8.3 %all-to-all-done = bf16[8,5,4,512]{3,2,1,0:T(4,128)(2,1)S(1)} async-done(((bf16[8,5,4,512]{3,2,1,0:T(4,128)(2,1)}), bf16[8,5,4,512]{3,2,1,0:T(4,128)(2,1)S(1)}, u32[]{:S(2)}, u32[]{:S(2)}) %all-to-all-start) | async-done | bytes 163872 | tf_op jit(solution)/shard_map/all_to_all | solution.py:30
  26.5 0.1 copy.18
  26.6 0.1 copy.20
  26.7 0.2 multiply_reduce_fusion
  26.9 0.4 convolution_bitcast_fusion
  27.3 0.1 reshape.135
  27.4 0.1 select_maximum_fusion
  27.5 0.6 broadcast_in_dim.4
  28.1 5.8 %all-to-all-start.1 = ((f32[8,8,128]{2,1,0:T(8,128)}), f32[8,8,128]{2,1,0:T(8,128)S(1)}, u32[]{:S(2)}, u32[]{:S(2)}) async-start(f32[8,8,128]{2,1,0:T(8,128)} %broadcast_in_dim.4), calls=%async_computation.1 | async-start | bytes 65536 | tf_op jit(solution)/shard_map/all_to_all | solution.py:30
  33.9 0.1 fusion
  34.0 0.2 pad_maximum_fusion
  34.1 0.1 pad.23.rhs_ref
  34.2 4.5 %all-to-all-done.1.sums_ref = f32[8,8,128]{2,1,0:T(8,128)S(1)} async-done(((f32[8,8,128]{2,1,0:T(8,128)}), f32[8,8,128]{2,1,0:T(8,128)S(1)}, u32[]{:S(2)}, u32[]{:S(2)}) %all-to-all-start.1) | async-done | bytes 32800 | tf_op jit(solution)/shard_map/all_to_all | solution.py:30
  38.7 6.7 %backward.1 = (bf16[5,512,1024]{2,1,0:T(8,128)(2,1)}, s16[32,72,128]{2,1,0:T(8,128)(2,1)S(1)}) custom-call(bf16[5,512,256]{2,1,0:T(8,128)(2,1)S(1)} %get-tuple-element.28.x_ref, bf16[256,1024]{1,0:T(8,128)(2,1)S(1)} %get-tuple-element.29.w_ref, f32[1,1024]{1,0:T(1,128)S(1)} %get-tuple-element.30.b_ref, bf16[4,1024]{1,0:T(4,128)(2,1)S(1)} %get-tuple-element.31.wo_ref, ...), custom_call_target="tpu_custom_call" | custom-call | tf_op jit(solution)/shard_map/backward/pallas_call | solution.py:223
  45.4 23.4 %all_to_all.25.in_ref = s16[32,72,128]{2,1,0:T(8,128)(2,1)S(1)} all-to-all(s16[32,72,128]{2,1,0:T(8,128)(2,1)S(1)} %get-tuple-element.34), channel_id=1, replica_groups=mesh['mem'=8,'band'=4,'yl'=2,'x'=4,'rep'=2] {'band','yl','x'}, dimensions={0} | all-to-all | bytes 1179648 | tf_op jit(solution)/shard_map/all_to_all | solution.py:30
  68.8 0.3 lat_sum.1
  69.1 12.2 %all_to_all.26.in_ref = s16[8,72,128]{2,1,0:T(8,128)(2,1)S(1)} all-to-all(s16[8,72,128]{2,1,0:T(8,128)(2,1)S(1)} %lat_sum.1), channel_id=1, replica_groups=mesh['mem'=8,'band'=4,'yl'=2,'x'=4,'rep'=2] {'mem'}, dimensions={0} | all-to-all | bytes 294912 | tf_op jit(solution)/shard_map/all_to_all | solution.py:30
  81.3 1.1 %mem_sum.1 = s16[32,72,128]{2,1,0:T(8,128)(2,1)} custom-call(s16[8,72,128]{2,1,0:T(8,128)(2,1)S(1)} %all_to_all.26.in_ref), custom_call_target="tpu_custom_call" | custom-call | tf_op jit(solution)/shard_map/mem_sum/pallas_call | solution.py:272
  82.4 5.2 %all-to-all-start.4 = ((s16[32,72,128]{2,1,0:T(8,128)(2,1)}), s16[32,72,128]{2,1,0:T(8,128)(2,1)S(1)}, u32[]{:S(2)}, u32[]{:S(2)}) async-start(s16[32,72,128]{2,1,0:T(8,128)(2,1)} %mem_sum.1), calls=%async_computation.4 | async-start | bytes 1179648 | tf_op jit(solution)/shard_map/all_to_all | solution.py:30
  87.7 6.1 %d_latent.1 = bf16[5,512,256]{2,1,0:T(8,128)(2,1)} custom-call(bf16[5,512,1024]{2,1,0:T(8,128)(2,1)} %get-tuple-element.33.dp_ref, bf16[256,1024]{1,0:T(8,128)(2,1)S(1)} %get-tuple-element.29.w_ref), custom_call_target="tpu_custom_call" | custom-call | tf_op jit(solution)/shard_map/d_latent/pallas_call | solution.py:250
  93.7 9.2 %all-to-all-done.4.in_ref = s16[32,72,128]{2,1,0:T(8,128)(2,1)S(1)} async-done(((s16[32,72,128]{2,1,0:T(8,128)(2,1)}), s16[32,72,128]{2,1,0:T(8,128)(2,1)S(1)}, u32[]{:S(2)}, u32[]{:S(2)}) %all-to-all-start.4) | async-done | bytes 589856 | tf_op jit(solution)/shard_map/all_to_all | solution.py:30
  103.0 1.2 %outputs.1 = (f32[256,1024]{1,0:T(8,128)}, f32[4,1024]{1,0:T(4,128)}, f32[1024]{0:T(1024)}, f32[4]{0:T(128)}) custom-call(s16[32,72,128]{2,1,0:T(8,128)(2,1)S(1)} %all-to-all-done.4.in_ref), custom_call_target="tpu_custom_call" | custom-call | tf_op jit(solution)/shard_map/outputs/pallas_call | solution.py:298
  (19 shorter events, 0.2 us)
Async XLA Ops:
  0.6 16.1 %copy-start.1 = (s32[512]{0:T(512)S(1)}, s32[512]{0:T(512)}, u32[]{:S(2)}) copy-start(s32[512]{0:T(512)} %param.15) | copy-start | bytes 6148
  0.6 17.1 %copy-start = (f32[4,512]{1,0:T(4,128)S(1)}, f32[4,512]{1,0:T(4,128)}, u32[]{:S(2)}) copy-start(f32[4,512]{1,0:T(4,128)} %param.14) | copy-start | bytes 24580
  6.4 20.1 %all-to-all-start = ((bf16[8,5,4,512]{3,2,1,0:T(4,128)(2,1)}), bf16[8,5,4,512]{3,2,1,0:T(4,128)(2,1)S(1)}, u32[]{:S(2)}, u32[]{:S(2)}) async-start(bf16[8,5,4,512]{3,2,1,0:T(4,128)(2,1)} %get-tuple-element.32), calls=%async_computation | async-start | bytes 327680 | tf_op jit(solution)/shard_map/all_to_all | solution.py:30
  28.1 10.6 %all-to-all-start.1 = ((f32[8,8,128]{2,1,0:T(8,128)}), f32[8,8,128]{2,1,0:T(8,128)S(1)}, u32[]{:S(2)}, u32[]{:S(2)}) async-start(f32[8,8,128]{2,1,0:T(8,128)} %broadcast_in_dim.4), calls=%async_computation.1 | async-start | bytes 65536 | tf_op jit(solution)/shard_map/all_to_all | solution.py:30
  82.4 20.5 %all-to-all-start.4 = ((s16[32,72,128]{2,1,0:T(8,128)(2,1)}), s16[32,72,128]{2,1,0:T(8,128)(2,1)S(1)}, u32[]{:S(2)}, u32[]{:S(2)}) async-start(s16[32,72,128]{2,1,0:T(8,128)(2,1)} %mem_sum.1), calls=%async_computation.4 | async-start | bytes 1179648 | tf_op jit(solution)/shard_map/all_to_all | solution.py:30

commit v5 on v4

--- a/solution.py
+++ b/solution.py
@@ -364,7 +364,8 @@
     )
     d_latent = down(d_preact, in_weight)
     scale = 1.0 / (members * cells_here * n_lat) ** 0.5
-    payload = reduce_and_copy(exchange(payload, LAT), n_mem, 1.0, "lat_sum")
+    received, d_latent = lax.optimization_barrier((exchange(payload, LAT), d_latent))
+    payload = reduce_and_copy(received, n_mem, 1.0, "lat_sum")
     payload = reduce_and_copy(exchange(payload, "mem"), n_lat, scale, "mem_sum")
     return (d_latent, *spread_out(exchange(payload, LAT), width, hid, nvars))
 

time: 105 us -> 105 us (level)
  starting transfers between devices: 21.3 us -> 24.5 us
  blocking collectives: 35.6 us -> 32.5 us
    all_to_all x3, starting transfers between devices: 21.3 us -> 24.5 us  [exchange(): return lax.all_to_all(blocks, axes, 0, 0)]
    all_to_all x2, blocking collectives: 35.6 us -> 32.5 us  [exchange(): return lax.all_to_all(blocks, axes, 0, 0)]
where the time goes in v5:
time: 105 us; the launch traced here: 104 us
  blocking collectives  32.5 us (31%)
  starting transfers between devices  24.5 us (23%)
  waiting for transfers between devices  22 us (21%)
  Pallas kernels  21 us (20%)
  local copies, waits for them, and re-layouts  2.05 us (2%)
    all_to_all x2, blocking collectives, exchange(): return lax.all_to_all(blocks, axes, 0, 0)  32.5 us
    all_to_all x3, starting transfers between devices, exchange(): return lax.all_to_all(blocks, axes, 0, 0)  24.5 us
    all_to_all x3, waiting for transfers between devices, exchange(): return lax.all_to_all(blocks, axes, 0, 0)  22 us
    pallas_call x1, Pallas kernels, backward(): pl.pallas_call(functools.partial(backward_kernel, entries, n_members), in...  7.48 us
    pallas_call x1, Pallas kernels, down(): pl.pallas_call(down_kernel, grid=(members,), in_specs=[member_block(cells...  6.07 us
    pallas_call x1, Pallas kernels, forward(): pl.pallas_call(field_kernel, in_specs=[in_hbm] * 5, out_shape=[jax.ShapeD...  5.69 us
  transfers between devices with their start and end apart: 3, of which 3 were waited for; matrix products, arithmetic and copies ran while one was open for 2% of the time, Pallas kernels for 6%

profile of v5, /device:TPU:8, one launch (start us, length us, event | category | flops | bytes accessed | tf_op | source)
XLA Modules:
  0.0 104.1 jit_solution(4141143453045664285)
XLA Ops:
  0.6 0.0 copy-start.1
  0.6 0.0 copy-start
  0.7 5.7 %field.1 = (bf16[8,5,4,512]{3,2,1,0:T(4,128)(2,1)}, bf16[5,512,256]{2,1,0:T(8,128)(2,1)S(1)}, bf16[256,1024]{1,0:T(8,128)(2,1)S(1)}, f32[1,1024]{1,0:T(1,128)S(1)}, bf16[4,1024]{1,0:T(4,128)(2,1)S(1)}) custom-call(bf16[5,512,256]{2,1,0:T(8,128)(2,1)} %x_hbm.1, bf16[256,1024]{1,0:T(8,128)(2,1)} %w_hbm.1, f32[1,1024]{1,0:T(1,128)} %bitcast.37, ...), custom_call_target="tpu_custom_call" | custom-call | tf_op jit(solution)/shard_map/field/pallas_call | solution.py:111
  6.4 10.3 %all-to-all-start = ((bf16[8,5,4,512]{3,2,1,0:T(4,128)(2,1)}), bf16[8,5,4,512]{3,2,1,0:T(4,128)(2,1)S(1)}, u32[]{:S(2)}, u32[]{:S(2)}) async-start(bf16[8,5,4,512]{3,2,1,0:T(4,128)(2,1)} %get-tuple-element.34), calls=%async_computation | async-start | bytes 327680 | tf_op jit(solution)/shard_map/all_to_all | solution.py:30
  16.7 0.0 copy-done.1
  16.8 1.0 copy.16
  17.8 0.0 copy-done
  17.9 0.1 fusion.8.keep_ref
  18.0 0.1 fusion.4
  18.1 8.3 %all-to-all-done = bf16[8,5,4,512]{3,2,1,0:T(4,128)(2,1)S(1)} async-done(((bf16[8,5,4,512]{3,2,1,0:T(4,128)(2,1)}), bf16[8,5,4,512]{3,2,1,0:T(4,128)(2,1)S(1)}, u32[]{:S(2)}, u32[]{:S(2)}) %all-to-all-start) | async-done | bytes 163872 | tf_op jit(solution)/shard_map/all_to_all | solution.py:30
  26.5 0.1 copy.18
  26.6 0.1 copy.20
  26.7 0.2 multiply_reduce_fusion
  26.9 0.4 convolution_bitcast_fusion
  27.3 0.1 reshape.135
  27.4 0.1 select_maximum_fusion
  27.5 0.6 broadcast_in_dim.4
  28.1 5.8 %all-to-all-start.1 = ((f32[8,8,128]{2,1,0:T(8,128)}), f32[8,8,128]{2,1,0:T(8,128)S(1)}, u32[]{:S(2)}, u32[]{:S(2)}) async-start(f32[8,8,128]{2,1,0:T(8,128)} %broadcast_in_dim.4), calls=%async_computation.1 | async-start | bytes 65536 | tf_op jit(solution)/shard_map/all_to_all | solution.py:30
  33.9 0.1 fusion
  34.0 0.2 pad_maximum_fusion
  34.1 0.1 pad.23.rhs_ref
  34.2 4.5 %all-to-all-done.1.sums_ref = f32[8,8,128]{2,1,0:T(8,128)S(1)} async-done(((f32[8,8,128]{2,1,0:T(8,128)}), f32[8,8,128]{2,1,0:T(8,128)S(1)}, u32[]{:S(2)}, u32[]{:S(2)}) %all-to-all-start.1) | async-done | bytes 32800 | tf_op jit(solution)/shard_map/all_to_all | solution.py:30
  38.7 7.5 %backward.1 = (bf16[5,512,1024]{2,1,0:T(8,128)(2,1)}, s16[32,72,128]{2,1,0:T(8,128)(2,1)}) custom-call(bf16[5,512,256]{2,1,0:T(8,128)(2,1)S(1)} %get-tuple-element.30.x_ref, bf16[256,1024]{1,0:T(8,128)(2,1)S(1)} %get-tuple-element.31.w_ref, f32[1,1024]{1,0:T(1,128)S(1)} %get-tuple-element.32.b_ref, bf16[4,1024]{1,0:T(4,128)(2,1)S(1)} %get-tuple-element.33.wo_ref, ...), custom_call_target="tpu_custom_call" | custom-call | tf_op jit(solution)/shard_map/backward/pallas_call | solution.py:223
  46.2 8.4 %all-to-all-start.2 = ((s16[32,72,128]{2,1,0:T(8,128)(2,1)}), s16[32,72,128]{2,1,0:T(8,128)(2,1)S(1)}, u32[]{:S(2)}, u32[]{:S(2)}) async-start(s16[32,72,128]{2,1,0:T(8,128)(2,1)} %get-tuple-element.35), calls=%async_computation.2 | async-start | bytes 1179648 | tf_op jit(solution)/shard_map/all_to_all | solution.py:30
  54.6 6.1 %d_latent.1 = bf16[5,512,256]{2,1,0:T(8,128)(2,1)} custom-call(bf16[5,512,1024]{2,1,0:T(8,128)(2,1)} %get-tuple-element.36.dp_ref, bf16[256,1024]{1,0:T(8,128)(2,1)S(1)} %get-tuple-element.31.w_ref), custom_call_target="tpu_custom_call" | custom-call | tf_op jit(solution)/shard_map/d_latent/pallas_call | solution.py:250
  60.7 9.2 %all-to-all-done.2.in_ref = s16[32,72,128]{2,1,0:T(8,128)(2,1)S(1)} async-done(((s16[32,72,128]{2,1,0:T(8,128)(2,1)}), s16[32,72,128]{2,1,0:T(8,128)(2,1)S(1)}, u32[]{:S(2)}, u32[]{:S(2)}) %all-to-all-start.2) | async-done | bytes 589856 | tf_op jit(solution)/shard_map/all_to_all | solution.py:30
  69.8 0.3 lat_sum.1
  70.2 12.2 %all_to_all.25.in_ref = s16[8,72,128]{2,1,0:T(8,128)(2,1)S(1)} all-to-all(s16[8,72,128]{2,1,0:T(8,128)(2,1)S(1)} %lat_sum.1), channel_id=1, replica_groups=mesh['mem'=8,'band'=4,'yl'=2,'x'=4,'rep'=2] {'mem'}, dimensions={0} | all-to-all | bytes 294912 | tf_op jit(solution)/shard_map/all_to_all | solution.py:30
  82.4 0.3 mem_sum.1
  82.6 20.3 %all_to_all.26.in_ref = s16[32,72,128]{2,1,0:T(8,128)(2,1)S(1)} all-to-all(s16[32,72,128]{2,1,0:T(8,128)(2,1)S(1)} %mem_sum.1), channel_id=1, replica_groups=mesh['mem'=8,'band'=4,'yl'=2,'x'=4,'rep'=2] {'band','yl','x'}, dimensions={0} | all-to-all | bytes 1179648 | tf_op jit(solution)/shard_map/all_to_all | solution.py:30
  103.0 1.2 %outputs.1 = (f32[256,1024]{1,0:T(8,128)}, f32[4,1024]{1,0:T(4,128)}, f32[1024]{0:T(1024)}, f32[4]{0:T(128)}) custom-call(s16[32,72,128]{2,1,0:T(8,128)(2,1)S(1)} %all_to_all.26.in_ref), custom_call_target="tpu_custom_call" | custom-call | tf_op jit(solution)/shard_map/outputs/pallas_call | solution.py:298
  (19 shorter events, 0.2 us)
Async XLA Ops:
  0.6 16.1 %copy-start.1 = (s32[512]{0:T(512)S(1)}, s32[512]{0:T(512)}, u32[]{:S(2)}) copy-start(s32[512]{0:T(512)} %param.15) | copy-start | bytes 6148
  0.6 17.1 %copy-start = (f32[4,512]{1,0:T(4,128)S(1)}, f32[4,512]{1,0:T(4,128)}, u32[]{:S(2)}) copy-start(f32[4,512]{1,0:T(4,128)} %param.14) | copy-start | bytes 24580
  6.4 20.1 %all-to-all-start = ((bf16[8,5,4,512]{3,2,1,0:T(4,128)(2,1)}), bf16[8,5,4,512]{3,2,1,0:T(4,128)(2,1)S(1)}, u32[]{:S(2)}, u32[]{:S(2)}) async-start(bf16[8,5,4,512]{3,2,1,0:T(4,128)(2,1)} %get-tuple-element.34), calls=%async_computation | async-start | bytes 327680 | tf_op jit(solution)/shard_map/all_to_all | solution.py:30
  28.1 10.6 %all-to-all-start.1 = ((f32[8,8,128]{2,1,0:T(8,128)}), f32[8,8,128]{2,1,0:T(8,128)S(1)}, u32[]{:S(2)}, u32[]{:S(2)}) async-start(f32[8,8,128]{2,1,0:T(8,128)} %broadcast_in_dim.4), calls=%async_computation.1 | async-start | bytes 65536 | tf_op jit(solution)/shard_map/all_to_all | solution.py:30
  46.2 23.6 %all-to-all-start.2 = ((s16[32,72,128]{2,1,0:T(8,128)(2,1)}), s16[32,72,128]{2,1,0:T(8,128)(2,1)S(1)}, u32[]{:S(2)}, u32[]{:S(2)}) async-start(s16[32,72,128]{2,1,0:T(8,128)(2,1)} %get-tuple-element.35), calls=%async_computation.2 | async-start | bytes 1179648 | tf_op jit(solution)/shard_map/all_to_all | solution.py:30
